TPU v7x, 512 devices: a whole 4x4x16 slice. The times are simulated.
512 devices in a mesh: face: 64 (over y, x, z_hi, core), band: 8 (over z_lo).
Axes of the slice: x: 4, y: 4, z: 16 (z_hi: 2, z_lo: 8; z = z_hi * 8 + z_lo), core: 2. Of those that a mesh axis runs over, the one named last changes fastest.
Arguments:
- code_ids: int32 [8, 256, 1024], P('band', None, 'face'), may hold values from 0 to 63999, as said below
- projection: float32 [6, 96], replicated, may hold values from -2.5 to 2.5
- first_weight: bfloat16 [9, 96, 96], replicated, may hold values from -0.21875 to 0.21875
- second_weight: bfloat16 [9, 96, 96], replicated, may hold values from -0.21875 to 0.21875
- norm_gain: float32 [96], replicated, may hold values from 0.5 to 1.5
- norm_shift: float32 [96], replicated, may hold values from -3 to 3
- cotangent: bfloat16 [1024, 768, 256], P('face', 'band'), may hold values from -0.009765625 to 0.009765625
Outputs:
- mixed: bfloat16 [1024, 768, 256], P('face', 'band')
- first_grad: float32 [9, 96, 96], P(None, 'band')
- second_grad: float32 [9, 96, 96], P(None, 'band')
- gain_grad: float32 [96], replicated
- shift_grad: float32 [96], replicated
- projection_grad: float32 [6, 96], replicated
Inputs may be any that keep to these rules, and one draw needn't show every extreme that they name: `code_ids`: six-digit mixed-radix codes, digits of 8, 8, 8, 5, 5, 5 levels, lowest digit first.
All inputs are finite; a program needn't handle non-finite values.
Results may differ from a plain program's by a relative error of at most 0.013.
Values may be sent and summed in bfloat16 or wider, within the bound.
A program may use at most 64 MiB of HBM per device.

v0:
```python
import jax
import jax.numpy as jnp
from jax import lax
from jax.sharding import PartitionSpec as P

GROUPS = 32


code_levels = (8, 8, 8, 5, 5, 5)
code_strides = (1, 8, 64, 512, 2560, 12800)


def extended(block, sides, width):
    for axis, dim in sides:
        count = lax.axis_size(axis)
        forward = [(i, i + 1) for i in range(count - 1)]
        forward.append((count - 1, 0))
        backward = [(target, source) for source, target in forward]
        low = lax.ppermute(
            lax.slice_in_dim(block, block.shape[dim] - width, None, axis=dim), axis, forward
        )
        high = lax.ppermute(lax.slice_in_dim(block, 0, width, axis=dim), axis, backward)
        block = jnp.concatenate([low, block, high], axis=dim)
    return block


def decode(code_ids):
    values = []
    for level_count, stride in zip(code_levels, code_strides):
        digits = code_ids // stride % level_count
        values.append((2.0 * digits.astype(jnp.float32) - (level_count - 1)) / level_count)
    return jnp.stack(values)


def surround(field):
    frames, channels, row_count, col_count = field.shape
    widened = extended(field, (("face", 3),), 1)
    framed = jnp.pad(widened, ((0, 0), (0, 0), (1, 1), (0, 0)))
    flattened = framed.reshape(frames, channels, (row_count + 2) * (col_count + 2))
    return jnp.pad(flattened, ((0, 0), (0, 0), (0, 2)))


def window(flattened, start, length):
    return lax.slice_in_dim(flattened, start, start + length, axis=2)


def conv_ahead(flattened, weights, row_count, col_count):
    stride = col_count + 2
    summed = None
    for tap_index in range(9):
        moved = window(flattened, tap_index // 3 * stride + tap_index % 3, row_count * stride)
        contribution = jnp.einsum(
            "fiq,io->foq", moved, weights[tap_index], preferred_element_type=jnp.float32
        )
        summed = contribution if summed is None else summed + contribution
    return summed.reshape(summed.shape[0], summed.shape[1], row_count, stride)[..., :col_count]


def conv_behind(flattened, weights, row_count, col_count):
    stride = col_count + 2
    summed = None
    for tap_index in range(9):
        moved = window(
            flattened, (2 - tap_index // 3) * stride + (2 - tap_index % 3), row_count * stride
        )
        contribution = jnp.einsum(
            "foq,io->fiq", moved, weights[tap_index], preferred_element_type=jnp.float32
        )
        summed = contribution if summed is None else summed + contribution
    return summed.reshape(summed.shape[0], summed.shape[1], row_count, stride)[..., :col_count]


def weight_terms(flattened, grads):
    frames, channels, row_count, col_count = grads.shape
    stride = col_count + 2
    widened = jnp.pad(grads, ((0, 0), (0, 0), (0, 0), (0, 2))).reshape(
        frames, channels, row_count * stride
    )
    return jnp.stack(
        [
            jnp.einsum(
                "fiq,foq->io",
                window(flattened, tap_index // 3 * stride + tap_index % 3, row_count * stride),
                widened,
                preferred_element_type=jnp.float32,
            )
            for tap_index in range(9)
        ]
    )


def group_total(values):
    sums = values.reshape(GROUPS, -1).sum(axis=1)
    return jnp.repeat(sums, values.shape[0] // GROUPS)


def column(values):
    return values[None, :, None, None]


def body(code_ids, projection, first_weight, second_weight, norm_gain, norm_shift, cotangent):
    frames = code_ids.shape[0]
    col_count, merged, row_count = cotangent.shape
    channels = merged // frames
    cot_field = jnp.transpose(
        cotangent.reshape(col_count, frames, channels, row_count), (1, 2, 3, 0)
    )
    latent = decode(code_ids)
    lifted = jnp.einsum(
        "kfrc,ko->forc", latent, projection, precision=lax.Precision.HIGHEST
    ).astype(jnp.bfloat16)
    lifted_flat = surround(lifted)
    first_out = conv_ahead(lifted_flat, first_weight, row_count, col_count)
    count = float(
        channels
        // GROUPS
        * frames
        * row_count
        * col_count
        * lax.axis_size("face")
        * lax.axis_size("band")
    )
    channel_sums = lax.psum(jnp.sum(first_out, axis=(0, 2, 3)), ("face", "band"))
    mean = group_total(channel_sums) / count
    squares = lax.psum(jnp.sum((first_out - column(mean)) ** 2, axis=(0, 2, 3)), ("face", "band"))
    variance = group_total(squares) / count
    scale = 1.0 / jnp.sqrt(variance + 1e-05)
    standard = (first_out - column(mean)) * column(scale)
    pre_act = standard * column(norm_gain) + column(norm_shift)
    activated = jax.nn.silu(pre_act).astype(jnp.bfloat16)
    act_flat = surround(activated)
    second_out = conv_ahead(act_flat, second_weight, row_count, col_count)
    mixed_field = (lifted.astype(jnp.float32) + second_out).astype(jnp.bfloat16)
    mixed = jnp.transpose(mixed_field, (3, 0, 1, 2)).reshape(col_count, merged, row_count)
    cot_flat = surround(cot_field)
    second_part = weight_terms(act_flat, cot_field)
    act_grad = conv_behind(cot_flat, second_weight, row_count, col_count)
    sigma = jax.nn.sigmoid(pre_act)
    pre_grad = act_grad * sigma * (1.0 + pre_act * (1.0 - sigma))
    shift_grad, gain_grad = lax.psum(
        (jnp.sum(pre_grad, axis=(0, 2, 3)), jnp.sum(pre_grad * standard, axis=(0, 2, 3))),
        ("face", "band"),
    )
    first_mean = group_total(norm_gain * shift_grad) / count
    second_mean = group_total(norm_gain * gain_grad) / count
    in_grad = (
        column(scale)
        * (pre_grad * column(norm_gain) - column(first_mean) - standard * column(second_mean))
    ).astype(jnp.bfloat16)
    in_flat = surround(in_grad)
    first_part = weight_terms(lifted_flat, in_grad)
    lifted_grad = cot_field.astype(jnp.float32) + conv_behind(
        in_flat, first_weight, row_count, col_count
    )
    proj_part = jnp.einsum("kfrc,forc->ko", latent, lifted_grad, precision=lax.Precision.HIGHEST)
    first_total, second_total, projection_grad = lax.psum(
        (first_part, second_part, proj_part), ("face", "band")
    )
    piece = channels // lax.axis_size("band")
    offset = lax.axis_index("band") * piece
    first_grad = lax.dynamic_slice_in_dim(first_total, offset, piece, 1)
    second_grad = lax.dynamic_slice_in_dim(second_total, offset, piece, 1)
    return (mixed, first_grad, second_grad, gain_grad, shift_grad, projection_grad)


def solution(mesh):
    return jax.shard_map(
        body,
        mesh=mesh,
        in_specs=(P("band", None, "face"), P(), P(), P(), P(), P(), P("face", "band", None)),
        out_specs=(
            P("face", "band", None),
            P(None, "band", None),
            P(None, "band", None),
            P(),
            P(),
            P(),
        ),
        check_vma=False,
    )
```

profile of v0, /device:TPU:1, one launch (start us, length us, event | category | flops | bytes accessed | tf_op | source)
XLA Modules:
  0.0 956.7 jit_solution(12957849166333498612)
XLA Ops:
  7.2 1.5 fusion.184
  10.4 16.8 %collective-permute-start = (bf16[1,96,256,1]{2,1,3,0:T(8,128)(2,1)S(1)}, bf16[1,96,256,1]{2,1,3,0:T(8,128)(2,1)S(1)}, u32[]{:S(2)}, u32[]{:S(2)}) collective-permute-start(bf16[1,96,256,1]{2,1,3,0:T(8,128)(2,1)S(1)} %get-tuple-element.20), channel_id=1, source_target_pairs={{0,8},{8,16},{16,24},{24,32},{32,40},{40,48},{48,56},{56,64},{64,7... | collective-permute-start | bytes 147464 | tf_op jit(solution)/shard_map/ppermute | solution.py:19
  27.2 1.9 collective-permute-start.1
  31.1 12.3 %collective-permute-start.4 = (bf16[1,96,256,1]{1,3,2,0:T(2,128)(2,1)}, bf16[1,96,256,1]{1,3,2,0:T(2,128)(2,1)}, u32[]{:S(2)}, u32[]{:S(2)}) collective-permute-start(bf16[1,96,256,1]{1,3,2,0:T(2,128)(2,1)} %get-tuple-element.16), channel_id=1, source_target_pairs={{0,8},{8,16},{16,24},{24,32},{32,40},{40,48},{48,56},{56,64},{64,7... | collective-permute-start | bytes 147464 | tf_op jit(solution)/shard_map/ppermute | solution.py:19
  43.5 1.9 collective-permute-start.5
  49.1 1.5 pad.33.clone
  50.5 2.5 reshape.394
  57.6 1.9 fusion
  59.5 3.0 copy.31
  62.5 3.6 reshape.404
  66.1 2.2 slice_reduce_fusion
  68.4 107.4 %psum.49 = f32[32,3]{1,0:T(8,128)S(1)} all-reduce(f32[32,3]{1,0:T(8,128)S(1)} %reshape.405), channel_id=1, replica_groups=mesh['face'=64,'band'=8] {'face','band'}, use_global_device_ids=true, to_apply=%region_1.2 | all-reduce | flops 96 | bytes 768 | tf_op jit(solution)/shard_map/psum | solution.py:123
  176.1 2.2 multiply_reduce_fusion.1
  178.4 100.7 %psum.50 = f32[32,3]{1,0:T(8,128)S(1)} all-reduce(f32[32,3]{1,0:T(8,128)S(1)} %reshape.406), channel_id=1, replica_groups=mesh['face'=64,'band'=8] {'face','band'}, use_global_device_ids=true, to_apply=%region_4.5 | all-reduce | flops 96 | bytes 768 | tf_op jit(solution)/shard_map/psum | solution.py:125
  279.4 3.1 select_maximum_fusion.2
  282.5 2.4 reshape.420
  290.2 1.8 fusion.2
  291.9 3.0 copy.35
  294.9 3.7 reshape.430
  298.6 5.0 fusion.200
  303.6 100.3 %all-reduce.10 = (f32[96]{0:T(128)S(1)}, f32[96]{0:T(128)S(1)}) all-reduce(f32[96]{0:T(128)S(1)} %get-tuple-element.7, f32[96]{0:T(128)S(1)} %get-tuple-element.6), channel_id=1, replica_groups=mesh['face'=64,'band'=8] {'face','band'}, use_global_device_ids=true, to_apply=%region_10.11 | all-reduce | flops 192 | bytes 1536 | tf_op jit(solution)/shard_map/psum | solution.py:140
  405.3 2.8 multiply_convert_fusion
  409.2 1.4 pad.39
  410.7 8.8 collective-permute-start.6
  419.4 1.9 collective-permute-start.7
  422.3 12.3 %collective-permute-start.2 = (bf16[1,96,256,1]{1,3,2,0:T(2,128)(2,1)}, bf16[1,96,256,1]{1,3,2,0:T(2,128)(2,1)S(1)}, u32[]{:S(2)}, u32[]{:S(2)}) collective-permute-start(bf16[1,96,256,1]{1,3,2,0:T(2,128)(2,1)} %get-tuple-element.18), channel_id=1, source_target_pairs={{0,8},{8,16},{16,24},{24,32},{32,40},{40,48},{48,56},{56,64},{64,7... | collective-permute-start | bytes 147464 | tf_op jit(solution)/shard_map/ppermute | solution.py:19
  434.6 2.1 collective-permute-start.3
  436.8 2.4 reshape.433
  444.7 3.1 select_maximum_fusion
  447.8 2.5 reshape.435
  454.6 1.8 fusion.3
  456.4 1.9 copy.36
  458.3 1.8 reshape.445
  460.1 3.3 fusion.5
  463.4 3.0 select_maximum_fusion.4
  466.4 2.7 reshape.407
  469.1 1.8 fusion.79
  475.5 2.2 convolution_add_fusion.23
  481.1 1.9 fusion.1
  483.0 3.3 fusion.71
  486.3 1.9 copy.32
  488.3 1.8 reshape.417
  490.0 1.6 slice-done
  491.6 1.7 copy.38
  493.3 109.8 %psum.55 = f32[6,96]{1,0:T(8,128)} all-reduce(f32[6,96]{1,0:T(8,128)S(1)} %fusion.71), channel_id=1, replica_groups=mesh['face'=64,'band'=8] {'face','band'}, use_global_device_ids=true, to_apply=%region_14.15 | all-reduce | flops 576 | bytes 4608 | tf_op jit(solution)/shard_map/psum | solution.py:156
  603.1 2.5 fusion.80
  605.6 342.2 %all-reduce.14.cloned.1.call-done = (f32[9,96,96]{2,1,0:T(8,128)}, f32[9,96,96]{2,1,0:T(8,128)}) async-done(((f32[9,96,96]{2,1,0:T(8,128)}, f32[9,96,96]{2,1,0:T(8,128)}), (f32[9,96,96]{2,1,0:T(8,128)}, f32[9,96,96]{2,1,0:T(8,128)})) %all-reduce.14.cloned.1.call-update) | async-done | bytes 663568 | tf_op jit(solution)/shard_map/psum | solution.py:156
  947.8 1.6 constant_dynamic-slice_fusion
  (135 shorter events, 38.9 us)
Async XLA Ops:
  7.2 1.7 copy-start
  7.2 22.0 %copy-start.15 = (bf16[16,96,256]{2,1,0:T(8,128)(2,1)S(1)}, bf16[16,96,256]{2,1,0:T(8,128)(2,1)}, u32[]{:S(2)}) copy-start(bf16[16,96,256]{2,1,0:T(8,128)(2,1)} %param.13) | copy-start | bytes 2359300
  7.2 940.6 %all-reduce.14.cloned.1.call-start = ((), (), s32[]{:S(2)}) async-start(), calls=%async_computation | async-start | bytes 1769472 | tf_op jit(solution)/shard_map/psum | solution.py:156
  8.9 18.3 %copy-start.9 = (f32[6,1,256,16]{2,0,3,1:T(8,128)}, f32[6,1,256,16]{2,0,3,1:T(8,128)S(1)}, u32[]{:S(2)}) copy-start(f32[6,1,256,16]{2,0,3,1:T(8,128)S(1)} %stack.87) | copy-start | bytes 294916
  10.4 36.7 %copy-start.5 = (bf16[1,96,256,16]{2,1,3,0:T(8,128)(2,1)}, bf16[1,96,256,16]{2,1,3,0:T(8,128)(2,1)S(1)}, u32[]{:S(2)}) copy-start(bf16[1,96,256,16]{2,1,3,0:T(8,128)(2,1)S(1)} %fusion.10) | copy-start | bytes 2359300
  10.4 36.7 %collective-permute-start = (bf16[1,96,256,1]{2,1,3,0:T(8,128)(2,1)S(1)}, bf16[1,96,256,1]{2,1,3,0:T(8,128)(2,1)S(1)}, u32[]{:S(2)}, u32[]{:S(2)}) collective-permute-start(bf16[1,96,256,1]{2,1,3,0:T(8,128)(2,1)S(1)} %get-tuple-element.20), channel_id=1, source_target_pairs={{0,8},{8,16},{16,24},{24,32},{32,40},{40,48},{48,56},{56,64},{64,7... | collective-permute-start | bytes 147464 | tf_op jit(solution)/shard_map/ppermute | solution.py:19
  27.2 19.8 %collective-permute-start.1 = (bf16[1,96,256,1]{2,1,3,0:T(8,128)(2,1)S(1)}, bf16[1,96,256,1]{2,1,3,0:T(8,128)(2,1)}, u32[]{:S(2)}, u32[]{:S(2)}) collective-permute-start(bf16[1,96,256,1]{2,1,3,0:T(8,128)(2,1)S(1)} %get-tuple-element.21), channel_id=1, source_target_pairs={{8,0},{16,8},{24,16},{32,24},{40,32},{48,40},{56,48},{64,56},{72,6... | collective-permute-start | bytes 147464 | tf_op jit(solution)/shard_map/ppermute | solution.py:22
  31.1 248.2 %collective-permute-start.4 = (bf16[1,96,256,1]{1,3,2,0:T(2,128)(2,1)}, bf16[1,96,256,1]{1,3,2,0:T(2,128)(2,1)}, u32[]{:S(2)}, u32[]{:S(2)}) collective-permute-start(bf16[1,96,256,1]{1,3,2,0:T(2,128)(2,1)} %get-tuple-element.16), channel_id=1, source_target_pairs={{0,8},{8,16},{16,24},{24,32},{32,40},{40,48},{48,56},{56,64},{64,7... | collective-permute-start | bytes 147464 | tf_op jit(solution)/shard_map/ppermute | solution.py:19
  43.5 235.9 %collective-permute-start.5 = (bf16[1,96,256,1]{1,3,2,0:T(2,128)(2,1)}, bf16[1,96,256,1]{1,3,2,0:T(2,128)(2,1)}, u32[]{:S(2)}, u32[]{:S(2)}) collective-permute-start(bf16[1,96,256,1]{1,3,2,0:T(2,128)(2,1)} %get-tuple-element.17), channel_id=1, source_target_pairs={{8,0},{16,8},{24,16},{32,24},{40,32},{48,40},{56,48},{64,56},{72,6... | collective-permute-start | bytes 147464 | tf_op jit(solution)/shard_map/ppermute | solution.py:22
  50.5 2.5 copy-start.11
  284.9 1.4 copy-start.13
  294.9 3.7 copy-start.18
  294.9 3.7 copy-start.19
  303.6 117.7 %copy-start.7 = (bf16[1,96,256,16]{1,3,2,0:T(8,128)(2,1)}, bf16[1,96,256,16]{1,3,2,0:T(8,128)(2,1)S(1)}, u32[]{:S(2)}) copy-start(bf16[1,96,256,16]{1,3,2,0:T(8,128)(2,1)S(1)} %get-tuple-element.13) | copy-start | bytes 2359300
  403.9 0.5 copy-start.21
  403.9 4.2 copy-start.20
  408.1 2.5 copy-start.3
  410.7 34.0 %collective-permute-start.6 = (bf16[1,96,256,1]{1,3,2,0:T(2,128)(2,1)}, bf16[1,96,256,1]{1,3,2,0:T(2,128)(2,1)}, u32[]{:S(2)}, u32[]{:S(2)}) collective-permute-start(bf16[1,96,256,1]{1,3,2,0:T(2,128)(2,1)} %get-tuple-element.14), channel_id=1, source_target_pairs={{0,8},{8,16},{16,24},{24,32},{32,40},{40,48},{48,56},{56,64},{64,7... | collective-permute-start | bytes 147464 | tf_op jit(solution)/shard_map/ppermute | solution.py:19
  419.4 25.3 %collective-permute-start.7 = (bf16[1,96,256,1]{1,3,2,0:T(2,128)(2,1)}, bf16[1,96,256,1]{1,3,2,0:T(2,128)(2,1)}, u32[]{:S(2)}, u32[]{:S(2)}) collective-permute-start(bf16[1,96,256,1]{1,3,2,0:T(2,128)(2,1)} %get-tuple-element.15), channel_id=1, source_target_pairs={{8,0},{16,8},{24,16},{32,24},{40,32},{48,40},{56,48},{64,56},{72,6... | collective-permute-start | bytes 147464 | tf_op jit(solution)/shard_map/ppermute | solution.py:22
  422.3 41.1 %collective-permute-start.2 = (bf16[1,96,256,1]{1,3,2,0:T(2,128)(2,1)}, bf16[1,96,256,1]{1,3,2,0:T(2,128)(2,1)S(1)}, u32[]{:S(2)}, u32[]{:S(2)}) collective-permute-start(bf16[1,96,256,1]{1,3,2,0:T(2,128)(2,1)} %get-tuple-element.18), channel_id=1, source_target_pairs={{0,8},{8,16},{16,24},{24,32},{32,40},{40,48},{48,56},{56,64},{64,7... | collective-permute-start | bytes 147464 | tf_op jit(solution)/shard_map/ppermute | solution.py:19
  434.6 28.7 %collective-permute-start.3 = (bf16[1,96,256,1]{1,3,2,0:T(2,128)(2,1)}, bf16[1,96,256,1]{1,3,2,0:T(2,128)(2,1)}, u32[]{:S(2)}, u32[]{:S(2)}) collective-permute-start(bf16[1,96,256,1]{1,3,2,0:T(2,128)(2,1)} %get-tuple-element.19), channel_id=1, source_target_pairs={{8,0},{16,8},{24,16},{32,24},{40,32},{48,40},{56,48},{64,56},{72,6... | collective-permute-start | bytes 147464 | tf_op jit(solution)/shard_map/ppermute | solution.py:22
  443.3 1.3 copy-start.4
  443.9 0.8 copy-start.16
  447.8 2.5 copy-start.12
  460.1 3.3 copy-start.8
  466.4 2.7 copy-start.14
  469.1 1.8 copy-start.2
  475.5 2.2 copy-start.17
  481.1 1.9 copy-start.10
  490.0 1.6 slice-start
  491.6 111.5 %copy-start.6 = (bf16[1,96,256,16]{2,1,3,0:T(8,128)(2,1)S(1)}, bf16[1,96,256,16]{2,1,3,0:T(8,128)(2,1)}, u32[]{:S(2)}) copy-start(bf16[1,96,256,16]{2,1,3,0:T(8,128)(2,1)} %copy-done.5) | copy-start | bytes 2359300
  493.3 456.1 %copy-start.1 = (f32[6,96]{1,0:T(8,128)S(1)}, f32[6,96]{1,0:T(8,128)}, u32[]{:S(2)}) copy-start(f32[6,96]{1,0:T(8,128)} %param.8) | copy-start | bytes 6916
Sparse Core Ops, SparseCore 0:
  483.1 464.6 all-reduce.13
where the time goes:
time: 966 us; the launch traced here: 957 us
  blocking collectives  418 us (43%)
  waiting for transfers between devices  342 us (35%)
  starting transfers between devices  58.2 us (6%)
  local copies, waits for them, and re-layouts  50.3 us (5%)
  matrix products  42.7 us (4%)
  other arithmetic  30.1 us (3%)
  between operations  15.1 us (2%)
    psum x1, waiting for transfers between devices, body(): lax.psum((first_part, second_part, proj_part), ('face', 'band'))  342 us
    psum x1, blocking collectives, body(): lax.psum((first_part, second_part, proj_part), ('face', 'band'))  110 us
    psum x1, blocking collectives, body(): lax.psum(jnp.sum(first_out, axis=(0, 2, 3)), ('face', 'band'))  107 us
    psum x1, blocking collectives, body(): lax.psum(jnp.sum((first_out - column(mean)) ** 2, axis=(0, 2, 3)), ('face...  101 us
    psum x1, blocking collectives, body(): lax.psum((jnp.sum(pre_grad, axis=(0, 2, 3)), jnp.sum(pre_grad * standard,...  100 us
    ppermute x4, starting transfers between devices, extended(): lax.ppermute(lax.slice_in_dim(block, block.shape[dim] - width, None, axis...  50.3 us
  transfers between devices with their start and end apart: 9, of which 1 were waited for; matrix products, arithmetic and copies ran while one was open for 7% of the time, Pallas kernels for 0%

commit v1 on v0

v1 whole, which is shorter than its diff:
```python
import jax
import jax.numpy as jnp
from jax import lax
from jax.experimental import pallas as pl
from jax.experimental.pallas import tpu as pltpu
from jax.sharding import PartitionSpec as P

MESH = pl.DeviceIdType.MESH
HIGHEST = lax.Precision.HIGHEST
F32, BF16 = jnp.float32, jnp.bfloat16

CH, ROWS, COLS = 96, 256, 16
PLANE, LINE, BANDS = 32, 16, 8
CHUNKS = 27
POSITIONS = float(2**21)
ONE = 46


def iota(shape, dim):
    return lax.broadcasted_iota(jnp.int32, shape, dim)


def dot(a, b):
    return lax.dot_general(a, b, (((1,), (0,)), ((), ())), preferred_element_type=F32)


def dot_t(a, b):
    return lax.dot_general(a, b, (((1,), (1,)), ((), ())), preferred_element_type=F32)


def dot32(a, b):
    return lax.dot_general(
        a, b, (((1,), (0,)), ((), ())), precision=HIGHEST, preferred_element_type=F32
    )


def dot32_t(a, b):
    return lax.dot_general(
        a, b, (((1,), (1,)), ((), ())), precision=HIGHEST, preferred_element_type=F32
    )


def pieces(value, count):
    parts = []
    for _ in range(count):
        part = value.astype(BF16).astype(F32)
        parts.append(part)
        value = value - part
    return parts


def later(value, lane):
    return jnp.where(lane == 0, 0.0, pltpu.roll(value, 1, 1))


def earlier(value, lane):
    return jnp.where(lane == ROWS - 1, 0.0, pltpu.roll(value, ROWS - 1, 1))


def unit_row(index):
    if index < 27:
        return index // 9 * 32 + index // 3 % 3 * 8 + index % 3 * 2
    return 96 + 2 * (index - 27) if index < 30 else ONE


def kernel(
    code_ref, proj_ref, w1_ref, w2_ref, gain_ref, shift_ref, cot_ref,
    mixed_ref, first_ref, second_ref, gain_out, shift_out, proj_out,
    own, edge_l, edge_r, halo_l, halo_r,
    digits, cots, acts, grads, w2p, w2t, back_w, ahead_w, p8, wt,
    gs, g_rs, g_z, g_ag, g_all,
    sg, sg_send, sg_recv, af, af_send, af_recv, z_send, z_recv, ag,
    halo_send_sem, halo_recv_sem, send_sem, recv_sem,
):
    face, band = lax.axis_index("face"), lax.axis_index("band")
    core, z_hi, yx = face % 2, face // 2 % 2, face // 4
    q, z = yx * 2 + core, z_hi * BANDS + band

    def plane(j):
        return (j // 2 * 4 + z_hi * 2 + j % 2, band)

    def line(j):
        return (yx * 4 + j // BANDS * 2 + core, j % BANDS)

    left, right = ((face + 63) % 64, band), ((face + 1) % 64, band)

    barrier = pltpu.get_barrier_semaphore()
    for target in (left, right):
        pl.semaphore_signal(barrier, 1, device_id=target, device_id_type=MESH)
    for j in range(PLANE):
        @pl.when(q != j)
        def _():
            pl.semaphore_signal(barrier, 1, device_id=plane(j), device_id_type=MESH)
    for j in range(LINE):
        @pl.when(z != j)
        def _():
            pl.semaphore_signal(barrier, 1, device_id=line(j), device_id_type=MESH)

    def send(src, dst, sem, target):
        return pltpu.make_async_remote_copy(
            src, dst, send_sem.at[sem], recv_sem.at[sem], device_id=target, device_id_type=MESH
        )

    lane = iota((8, ROWS), 1)
    wide = iota((CH, ROWS), 1)

    codes = jnp.transpose(code_ref[0].astype(F32))
    own[...] = codes
    edge_l[...] = codes[0:2]
    edge_r[...] = codes[COLS - 2 : COLS]

    place, channel = iota((CH, CH), 0), iota((CH, CH), 1)
    perm = (channel == place % 32 // 4 * 12 + place // 32 * 4 + place % 4).astype(BF16)
    eye = (channel == place).astype(BF16)
    same_group = (channel // 3 == place // 3).astype(F32)
    for dc in range(3):
        for dr in range(3):
            tap, at = dr * 3 + dc, dc * 3 + dr
            w2p[pl.ds(at * CH, CH), :] = dot(perm, w2_ref[tap]).astype(BF16)
            back = (2 - dc) * 3 + dr
            w2t[pl.ds(back * CH, CH), :] = dot_t(eye, w2p[pl.ds(at * CH, CH), :]).astype(BF16)
    ahead_w[...] = dot_t(eye, w2p[...]).astype(BF16)
    back_w[...] = dot_t(eye, w2t[...]).astype(BF16)

    pl.semaphore_wait(barrier, PLANE - 1 + LINE - 1 + 2)

    to_right = pltpu.make_async_remote_copy(
        edge_r, halo_l, halo_send_sem.at[0], halo_recv_sem.at[0], device_id=right, device_id_type=MESH
    )
    to_left = pltpu.make_async_remote_copy(
        edge_l, halo_r, halo_send_sem.at[1], halo_recv_sem.at[1], device_id=left, device_id_type=MESH
    )
    to_right.start()
    to_left.start()

    level = jnp.where(iota((8, 1), 0) < 3, 8.0, 5.0)
    p8[...] = jnp.zeros_like(p8)
    p8[0:6, 0:CH] = proj_ref[...] / level[0:6]
    proj8 = p8[:, 0:CH]
    proj_parts = pieces(proj8, 3)
    proj_rows = jnp.concatenate(proj_parts + [jnp.zeros_like(proj8)], axis=0).astype(BF16)
    for dc in range(3):
        for dr in range(3):
            got = dot(proj_rows, w1_ref[dr * 3 + dc])
            wt[pl.ds(dc * 32 + dr * 8, 8), :] = got[0:8] + got[8:16] + got[16:24]
        wt[pl.ds(dc * 32 + 24, 8), :] = jnp.zeros((8, CH), F32)
    no_rows = jnp.zeros_like(proj8)
    lift_w = jnp.concatenate(
        [
            dot_t(eye, jnp.concatenate([no_rows, part, no_rows, no_rows], axis=0).astype(BF16))
            for part in proj_parts
        ],
        axis=0,
    ).astype(BF16)

    cots[0:2] = jnp.zeros((2, 3, CH, ROWS), BF16)
    cots[COLS + 2 : COLS + 4] = jnp.zeros((2, 3, CH, ROWS), BF16)

    def cot_step(c, carry):
        value = cot_ref[c]
        wider = value.astype(F32)
        cots[c + 2, 0] = earlier(wider, wide).astype(BF16)
        cots[c + 2, 1] = value
        cots[c + 2, 2] = later(wider, wide).astype(BF16)
        return carry

    lax.fori_loop(0, COLS, cot_step, 0)

    to_right.wait()
    to_left.wait()

    index = iota((8, 1), 0)
    stride = jnp.where(
        index == 0, 1.0, jnp.where(index == 1, 8.0, jnp.where(index == 2, 64.0,
        jnp.where(index == 3, 512.0, jnp.where(index == 4, 2560.0, 12800.0)))))
    per_stride, per_level = 1.0 / stride, 1.0 / level
    for c in range(COLS + 4):
        if c < 2:
            row = halo_l[c : c + 1, :]
        elif c < COLS + 2:
            row = own[c - 2 : c - 1, :]
        else:
            row = halo_r[c - COLS - 2 : c - COLS - 1, :]
        quotient = jnp.floor((row + 0.5) * per_stride)
        digit = quotient - level * jnp.floor((quotient + 0.5) * per_level)
        value = jnp.where(index < 6, 2.0 * digit - (level - 1.0), 0.0)
        block = [later(value, lane), jnp.where(index == 6, 1.0, value), earlier(value, lane)]
        digits[c] = jnp.concatenate(block + [jnp.zeros_like(value)], axis=0).astype(BF16)
    digits[COLS + 4 : COLS + 8] = jnp.zeros((4, 32, ROWS), BF16)

    gram = None
    for c in range(COLS):
        term = dot_t(digits[c + 2], digits[c + 2 : c + 6].reshape(128, ROWS))
        gram = term if gram is None else gram + term
    for j in range(PLANE):
        gs[j] = gram[j : j + 1]
    for j in range(PLANE):
        @pl.when(q != j)
        def _():
            send(gs.at[j], g_rs.at[q], 0, plane(j)).start()
    g_rs[q] = gs[q]

    def grad_step(c, carry):
        grads[c] = dot(back_w[...], cots[pl.ds(c, 3)].reshape(9 * CH, ROWS))
        return carry

    lax.fori_loop(0, 6, grad_step, 0)
    some = send(gs.at[pl.ds(0, PLANE - 1)], g_rs.at[pl.ds(0, PLANE - 1)], 0, right)
    some.wait()
    g_z[z] = jnp.sum(g_rs[...], axis=0)
    for j in range(LINE):
        @pl.when(z != j)
        def _():
            send(g_z.at[z], g_z.at[z], 1, line(j)).start()
    lax.fori_loop(6, 12, grad_step, 0)
    send(g_z.at[pl.ds(0, LINE - 1)], g_z.at[pl.ds(0, LINE - 1)], 1, right).wait()
    g_ag[q] = jnp.sum(g_z[...], axis=0)
    for j in range(PLANE):
        @pl.when(q != j)
        def _():
            send(g_ag.at[q], g_ag.at[q], 2, plane(j)).start()
    lax.fori_loop(12, 18, grad_step, 0)
    send(g_ag.at[pl.ds(0, PLANE - 1)], g_ag.at[pl.ds(0, PLANE - 1)], 2, right).wait()
    for j in range(PLANE):
        g_all[j : j + 1, :] = g_ag[j]
    g_all[PLANE:128, :] = jnp.zeros((128 - PLANE, 128), F32)

    near = g_all[0:32, :]
    flipped = jnp.transpose(g_all[...])
    lane32 = iota((32, 128), 1)
    gram_all = jnp.concatenate(
        [
            near,
            jnp.where(lane32 < 32, flipped[32:64], pltpu.roll(near, 32, 1)),
            jnp.where(
                lane32 < 32,
                flipped[64:96],
                jnp.where(lane32 < 64, pltpu.roll(flipped[32:64], 32, 1), pltpu.roll(near, 64, 1)),
            ),
        ],
        axis=0,
    )[:, 0:CH]
    digit_sum = gram_all[:, ONE : ONE + 1]
    digit_mean = digit_sum / POSITIONS
    covariance = gram_all / POSITIONS - digit_mean * (gram_all[ONE : ONE + 1, :] / POSITIONS)
    weights = wt[...]
    spread = dot32(covariance, weights)

    def by_group(value):
        return dot32(jnp.broadcast_to(value, (8, CH)), same_group)[0:1]

    channel_mean = jnp.sum(weights * digit_mean, axis=0, keepdims=True)
    mean = by_group(channel_mean) / 3.0
    off = channel_mean - mean
    variance = by_group(jnp.sum(weights * spread, axis=0, keepdims=True) + off * off) / 3.0
    scale = 1.0 / jnp.sqrt(variance + 1e-05)
    gain = gain_ref[...]
    steep = scale * gain
    pre_w = jnp.where(place == ONE, shift_ref[...] - mean * steep, weights * steep)
    pre_w = jnp.concatenate(
        [dot_t(perm, part.astype(BF16)) for part in pieces(pre_w, 2)], axis=0
    ).astype(BF16)

    def act_step(c, total):
        taps = digits[pl.ds(c, 3)].reshape(CH, ROWS)
        both = dot(pre_w, taps)
        pre = both[0:CH] + both[CH : 2 * CH]
        sigma = 0.5 * jnp.tanh(0.5 * pre) + 0.5
        act = pre * sigma
        slope = sigma + act * (1.0 - sigma)
        acts[c, 0] = later(act, wide).astype(BF16)
        acts[c, 1] = act.astype(BF16)
        acts[c, 2] = earlier(act, wide).astype(BF16)
        return total + dot_t(taps, (grads[c] * slope).astype(BF16))

    total = lax.fori_loop(0, COLS + 2, act_step, jnp.zeros((CH, CH), F32))
    af[...] = jnp.zeros_like(af)
    af[0:CH, 0:CH] = dot32(total, perm.astype(F32))

    sg[...] = jnp.zeros_like(sg)

    def second_step(c, total):
        value = cot_ref[c]
        sg[:, 0:CH] += dot_t(acts[pl.ds(c, 3)].reshape(9 * CH, ROWS), value)
        return total + dot_t(digits[c + 2], value)

    cot_sum = lax.fori_loop(0, COLS, second_step, jnp.zeros((32, CH), F32))
    af[CH : CH + 8, 0:CH] = cot_sum[8:16]
    sg_send[...] = sg[...].reshape(CHUNKS, 32, 128).astype(BF16)
    for j in range(PLANE - 1):
        af_send[j] = af[unit_row(j) : unit_row(j) + 2, :]
    af_send[PLANE - 1] = jnp.zeros((2, 128), F32)

    for j in range(PLANE):
        @pl.when(q != j)
        def _():
            if j < CHUNKS:
                send(sg_send.at[j], sg_recv.at[q], 3, plane(j)).start()
            send(af_send.at[j], af_recv.at[q], 4, plane(j)).start()
    af_recv[q] = af_send[q]

    @pl.when(q < CHUNKS)
    def _():
        sg_recv[q] = sg_send[q]

    def mixed_step(c, carry):
        out = dot(ahead_w[...], acts[pl.ds(c, 3)].reshape(9 * CH, ROWS))
        lift = dot(lift_w, digits[c + 2])
        lift = (lift[0:CH] + lift[CH : 2 * CH]) + lift[2 * CH : 3 * CH]
        mixed_ref[c] = (lift.astype(BF16).astype(F32) + out).astype(BF16)
        return carry

    lax.fori_loop(0, 6, mixed_step, 0)
    z_send[...] = jnp.zeros_like(z_send)

    @pl.when(q < CHUNKS)
    def _():
        send(sg_send.at[pl.ds(0, CHUNKS - 1)], sg_recv.at[pl.ds(0, CHUNKS - 1)], 3, right).wait_send()
        send(sg_recv.at[pl.ds(0, PLANE - 1)], sg_recv.at[pl.ds(0, PLANE - 1)], 3, right).wait_recv()

        def add(j, total):
            return total + sg_recv[j].astype(F32)

        total = lax.fori_loop(0, PLANE, add, jnp.zeros((32, 128), F32))
        for b in range(BANDS):
            z_send[b, 0:4] = total[4 * b : 4 * b + 4]

    @pl.when(q >= CHUNKS)
    def _():
        send(sg_send, sg_recv.at[pl.ds(0, CHUNKS)], 3, right).wait_send()

    send(af_send.at[pl.ds(0, PLANE - 1)], af_recv.at[pl.ds(0, PLANE - 1)], 4, right).wait()
    af_sum = jnp.sum(af_recv[...], axis=0)
    for b in range(BANDS):
        z_send[b, 4:6] = af_sum

    for j in range(LINE):
        @pl.when(z != j)
        def _():
            send(z_send.at[j % BANDS], z_recv.at[z], 5, line(j)).start()
    z_recv[z] = z_send[band]
    lax.fori_loop(6, 12, mixed_step, 0)
    send(z_recv.at[pl.ds(0, LINE - 1)], z_recv.at[pl.ds(0, LINE - 1)], 5, right).wait()
    ag[q] = jnp.sum(z_recv[...], axis=0)
    for j in range(PLANE):
        @pl.when(q != j)
        def _():
            send(ag.at[q], ag.at[q], 6, plane(j)).start()
    lax.fori_loop(12, COLS, mixed_step, 0)
    send(ag.at[pl.ds(0, PLANE - 1)], ag.at[pl.ds(0, PLANE - 1)], 6, right).wait()

    for j in range(CHUNKS):
        tap = j // 3 % 3 * 3 + j // 9
        second_ref[tap, j % 3 * 4 : j % 3 * 4 + 4, :] = ag[j, 0:4, 0:CH]
    for j in range(PLANE - 1):
        af[unit_row(j) : unit_row(j) + 2, :] = ag[j, 4:6]

    sums = af[0:CH, 0:CH]
    shift_grad = af[ONE : ONE + 1, 0:CH]
    gain_grad = scale * (jnp.sum(weights * sums, axis=0, keepdims=True) - mean * shift_grad)
    shift_out[...] = shift_grad
    gain_out[...] = gain_grad
    count = 3.0 * POSITIONS
    first_mean = by_group(gain * shift_grad) / count
    second_mean = by_group(gain * gain_grad) / count
    standard_sum = scale * (POSITIONS * spread + digit_sum * off)
    grad_sum = scale * (gain * sums - first_mean * digit_sum - second_mean * standard_sum)

    chosen = iota((16, CH), 1) == band * 12 + iota((16, CH), 0)
    proj_band = dot32_t(chosen.astype(F32), proj8)
    back_sum = None
    for dc in range(3):
        for dr in range(3):
            part = grad_sum[dc * 32 + dr * 8 : dc * 32 + dr * 8 + 8]
            first_ref[dr * 3 + dc] = dot32(proj_band, part)[0:12]
            rows = jnp.concatenate(pieces(part, 3) + [no_rows], axis=0).astype(BF16)
            term = dot_t(rows, w1_ref[dr * 3 + dc])
            back_sum = term if back_sum is None else back_sum + term
    back_sum = back_sum[0:8] + back_sum[8:16] + back_sum[16:24] + af[CH : CH + 8, 0:CH]
    proj_out[...] = (back_sum / level)[0:6]


def body(code_ids, projection, first_weight, second_weight, norm_gain, norm_shift, cotangent):
    shape = jax.ShapeDtypeStruct
    vmem = pl.BlockSpec(memory_space=pltpu.VMEM)
    scratch = [
        pltpu.VMEM((COLS, ROWS), F32),
        pltpu.VMEM((2, ROWS), F32), pltpu.VMEM((2, ROWS), F32),
        pltpu.VMEM((2, ROWS), F32), pltpu.VMEM((2, ROWS), F32),
        pltpu.VMEM((COLS + 8, 32, ROWS), BF16),
        pltpu.VMEM((COLS + 4, 3, CH, ROWS), BF16),
        pltpu.VMEM((COLS + 2, 3, CH, ROWS), BF16),
        pltpu.VMEM((COLS + 2, CH, ROWS), F32),
        pltpu.VMEM((9 * CH, CH), BF16), pltpu.VMEM((9 * CH, CH), BF16),
        pltpu.VMEM((CH, 9 * CH), BF16), pltpu.VMEM((CH, 9 * CH), BF16),
        pltpu.VMEM((8, 128), F32), pltpu.VMEM((CH, CH), F32),
        pltpu.VMEM((PLANE, 1, 128), F32), pltpu.VMEM((PLANE, 1, 128), F32),
        pltpu.VMEM((LINE, 1, 128), F32), pltpu.VMEM((PLANE, 1, 128), F32),
        pltpu.VMEM((128, 128), F32),
        pltpu.VMEM((9 * CH, 128), F32),
        pltpu.VMEM((CHUNKS, 32, 128), BF16), pltpu.VMEM((PLANE, 32, 128), BF16),
        pltpu.VMEM((CH + 8, 128), F32),
        pltpu.VMEM((PLANE, 2, 128), F32), pltpu.VMEM((PLANE, 2, 128), F32),
        pltpu.VMEM((BANDS, 8, 128), F32), pltpu.VMEM((LINE, 8, 128), F32),
        pltpu.VMEM((PLANE, 8, 128), F32),
        pltpu.SemaphoreType.DMA((2,)), pltpu.SemaphoreType.DMA((2,)),
        pltpu.SemaphoreType.DMA((7,)), pltpu.SemaphoreType.DMA((7,)),
    ]
    mixed, first, second, gain_grad, shift_grad, proj = pl.pallas_call(
        kernel,
        out_shape=[
            shape((COLS, CH, ROWS), BF16),
            shape((9, 12, CH), F32),
            shape((9, 12, CH), F32),
            shape((1, CH), F32),
            shape((1, CH), F32),
            shape((6, CH), F32),
        ],
        in_specs=[vmem] * 7,
        out_specs=[vmem] * 6,
        scratch_shapes=scratch,
        compiler_params=pltpu.CompilerParams(
            collective_id=0, has_side_effects=True, vmem_limit_bytes=40 * 1024 * 1024
        ),
        cost_estimate=pl.CostEstimate(
            flops=2_500_000_000, bytes_accessed=2_500_000, transcendentals=450_000
        ),
    )(
        code_ids,
        projection,
        first_weight,
        second_weight,
        norm_gain.reshape(1, CH),
        norm_shift.reshape(1, CH),
        cotangent,
    )
    return mixed, first, second, gain_grad.reshape(CH), shift_grad.reshape(CH), proj


def solution(mesh):
    return jax.shard_map(
        body,
        mesh=mesh,
        in_specs=(P("band", None, "face"), P(), P(), P(), P(), P(), P("face", "band", None)),
        out_specs=(
            P("face", "band", None),
            P(None, "band", None),
            P(None, "band", None),
            P(),
            P(),
            P(),
        ),
        check_vma=False,
    )
```

time: 966 us -> 82 us (0.08)
  blocking collectives: 418 us -> 0 us
  waiting for transfers between devices: 342 us -> 0 us
  Pallas kernels: 0 us -> 73.4 us
  starting transfers between devices: 58.2 us -> 0 us
  matrix products: 42.7 us -> 0 us
  local copies, waits for them, and re-layouts: 50.3 us -> 7.61 us
  other arithmetic: 30.1 us -> 0 us
  between operations: 15.1 us -> 0.7 us
    psum x4 -> x0, blocking collectives: 418 us -> none  [the longest x1 110 us: body(): lax.psum((first_part, second_part, proj_part), ('face', 'band'))]
    psum x1 -> x0, waiting for transfers between devices: 342 us -> none  [body(): lax.psum((first_part, second_part, proj_part), ('face', 'band'))]
    pallas_call x0 -> x1, Pallas kernels: none -> 73.4 us  [body(): pl.pallas_call(kernel, out_shape=[shape((COLS, CH, ROWS), BF16), shape((9...]
    ppermute x8 -> x0, starting transfers between devices: 58.2 us -> none  [the longest x4 50.3 us: extended(): lax.ppermute(lax.slice_in_dim(block, block.shape[dim] - width, None, axis...]
    dot_general x56 -> x0, matrix products: 42.7 us -> none  [the longest x18 15.7 us: conv_ahead(): jnp.einsum('fiq,io->foq', moved, weights[tap_index], preferred_element_ty...]
    reshape x12 -> x0, local copies, waits for them, and re-layouts: 21.3 us -> none  [the longest x4 10 us: surround(): framed.reshape(frames, channels, (row_count + 2) * (col_count + 2))]
    concatenate x4 -> x0, other arithmetic: 10.1 us -> none  [extended(): block = jnp.concatenate([low, block, high], axis=dim)]
    add x4 -> x0, local copies, waits for them, and re-layouts: 9.9 us -> none  [the longest x2 4.95 us: conv_behind(): summed = contribution if summed is None else summed + contribution]
  transfers between devices with their start and end apart: 9 -> 0, of which waited for: 1 -> 0; matrix products, arithmetic and copies ran while one was open for 7% -> 0% of each run, Pallas kernels for 0% -> 0%
where the time goes in v1:
time: 82 us; the launch traced here: 81.7 us
  Pallas kernels  73.4 us (90%)
  local copies, waits for them, and re-layouts  7.61 us (9%)
    pallas_call x1, Pallas kernels, body(): pl.pallas_call(kernel, out_shape=[shape((COLS, CH, ROWS), BF16), shape((9...  73.4 us
    unnamed x19, local copies, waits for them, and re-layouts  7.61 us

profile of v1, /device:TPU:1, one launch (start us, length us, event | category | flops | bytes accessed | tf_op | source)
XLA Modules:
  0.0 81.7 jit_solution(16586802451523826357)
XLA Ops:
  0.6 0.0 copy-start.3
  0.6 0.0 copy-start.4
  0.7 0.0 copy-start.5
  0.7 0.8 %copy.13.code_ref = s32[1,256,16]{2,1,0:T(8,128)S(1)} copy(s32[1,256,16]{1,2,0:T(8,128)} %param.7) | data formatting | bytes 32768 | tf_op args[0]
  1.5 0.0 copy-done.3
  1.5 0.0 copy-done.4
  1.5 0.0 copy-done.5
  1.5 0.0 copy-start
  1.5 1.1 %copy-done = bf16[16,96,256]{2,1,0:T(8,128)(2,1)S(1)} copy-done((bf16[16,96,256]{2,1,0:T(8,128)(2,1)S(1)}, bf16[16,96,256]{2,1,0:T(8,128)(2,1)}, u32[]{:S(2)}) %copy-start) | copy-done | bytes 786456
  2.7 0.0 copy-start.1
  2.7 0.9 %copy-done.1 = bf16[9,96,96]{2,1,0:T(8,128)(2,1)S(1)} copy-done((bf16[9,96,96]{2,1,0:T(8,128)(2,1)S(1)}, bf16[9,96,96]{2,1,0:T(8,128)(2,1)}, u32[]{:S(2)}) %copy-start.1) | copy-done | bytes 165912
  3.6 0.0 copy-start.2
  3.6 0.9 %copy-done.2 = bf16[9,96,96]{2,1,0:T(8,128)(2,1)S(1)} copy-done((bf16[9,96,96]{2,1,0:T(8,128)(2,1)S(1)}, bf16[9,96,96]{2,1,0:T(8,128)(2,1)}, u32[]{:S(2)}) %copy-start.2) | copy-done | bytes 165912
  4.5 73.4 %shard_map.118 = (bf16[16,96,256]{2,1,0:T(8,128)(2,1)S(1)}, f32[9,12,96]{2,1,0:T(8,128)S(1)}, f32[9,12,96]{2,1,0:T(8,128)S(1)}, f32[1,96]{1,0:T(1,128)S(1)}, f32[1,96]{1,0:T(1,128)S(1)}, /*index=5*/f32[6,96]{1,0:T(8,128)S(1)}) custom-call(s32[1,256,16]{2,1,0:T(8,128)S(1)} %copy.13.code_ref, f32[6,96]{1,0:T(8,128)S(1)} %copy-done.3, ...), custom_call_target="tpu_custom_call" | custom-call | flops 2500000000 | bytes 2500000 | tf_op jit(solution)/shard_map/pallas_call | solution.py:409
  78.0 0.9 %copy.20 = bf16[16,96,256]{2,1,0:T(8,128)(2,1)} copy(bf16[16,96,256]{2,1,0:T(8,128)(2,1)S(1)} %get-tuple-element.24) | data formatting | bytes 1572864
  78.9 0.6 copy.21
  79.5 0.6 copy.22
  80.1 0.5 copy.23
  80.6 0.5 copy.24
  81.1 0.6 copy.25
Async XLA Ops:
  0.6 0.9 %copy-start.3 = (f32[6,96]{1,0:T(8,128)S(1)}, f32[6,96]{1,0:T(8,128)}, u32[]{:S(2)}) copy-start(f32[6,96]{1,0:T(8,128)} %proj_ref.1) | copy-start | bytes 6916
  0.6 0.9 %copy-start.4 = (f32[96]{0:T(128)S(1)}, f32[96]{0:T(128)}, u32[]{:S(2)}) copy-start(f32[96]{0:T(128)} %param.11) | copy-start | bytes 1156
  0.7 0.9 %copy-start.5 = (f32[96]{0:T(128)S(1)}, f32[96]{0:T(128)}, u32[]{:S(2)}) copy-start(f32[96]{0:T(128)} %param.12) | copy-start | bytes 1156
  1.5 1.1 %copy-start = (bf16[16,96,256]{2,1,0:T(8,128)(2,1)S(1)}, bf16[16,96,256]{2,1,0:T(8,128)(2,1)}, u32[]{:S(2)}) copy-start(bf16[16,96,256]{2,1,0:T(8,128)(2,1)} %cot_ref.1) | copy-start | bytes 2359300
  2.7 0.9 %copy-start.1 = (bf16[9,96,96]{2,1,0:T(8,128)(2,1)S(1)}, bf16[9,96,96]{2,1,0:T(8,128)(2,1)}, u32[]{:S(2)}) copy-start(bf16[9,96,96]{2,1,0:T(8,128)(2,1)} %w1_ref.1) | copy-start | bytes 497668
  3.6 0.9 %copy-start.2 = (bf16[9,96,96]{2,1,0:T(8,128)(2,1)S(1)}, bf16[9,96,96]{2,1,0:T(8,128)(2,1)}, u32[]{:S(2)}) copy-start(bf16[9,96,96]{2,1,0:T(8,128)(2,1)} %w2_ref.1) | copy-start | bytes 497668

commit v2 on v1

--- a/solution.py
+++ b/solution.py
@@ -13,6 +13,7 @@
 PLANE, LINE, BANDS = 32, 16, 8
 CHUNKS = 27
 POSITIONS = float(2**21)
+VMEM_BYTES = 64 * 1024 * 1024 - 65536
 ONE = 46
 
 
@@ -64,14 +65,27 @@
 
 
 def kernel(
-    code_ref, proj_ref, w1_ref, w2_ref, gain_ref, shift_ref, cot_ref,
-    mixed_ref, first_ref, second_ref, gain_out, shift_out, proj_out,
+    code_in, proj_in, w1_in, w2_in, gain_in, shift_in, cot_in,
+    mixed_out, first_ref, second_ref, gain_out, shift_out, proj_out,
+    code_ref, proj_ref, w1_ref, w2_ref, gain_ref, shift_ref, cot_ref, mixed_ref,
     own, edge_l, edge_r, halo_l, halo_r,
     digits, cots, acts, grads, w2p, w2t, back_w, ahead_w, p8, wt,
     gs, g_rs, g_z, g_ag, g_all,
-    sg, sg_send, sg_recv, af, af_send, af_recv, z_send, z_recv, ag,
-    halo_send_sem, halo_recv_sem, send_sem, recv_sem,
+    sg_send, sg_recv, af, af_send, af_recv, z_send, z_recv, ag,
+    in_sem, out_sem, halo_send_sem, halo_recv_sem, send_sem, recv_sem,
 ):
+    arrivals = [
+        pltpu.make_async_copy(source, target, in_sem.at[k])
+        for k, (source, target) in enumerate(
+            [
+                (code_in, code_ref), (proj_in, proj_ref), (w1_in, w1_ref), (w2_in, w2_ref),
+                (gain_in, gain_ref), (shift_in, shift_ref), (cot_in, cot_ref),
+            ]
+        )
+    ]
+    for arrival in arrivals:
+        arrival.start()
+
     face, band = lax.axis_index("face"), lax.axis_index("band")
     core, z_hi, yx = face % 2, face // 2 % 2, face // 4
     q, z = yx * 2 + core, z_hi * BANDS + band
@@ -104,10 +118,25 @@
     lane = iota((8, ROWS), 1)
     wide = iota((CH, ROWS), 1)
 
-    codes = jnp.transpose(code_ref[0].astype(F32))
+    arrivals[0].wait()
+    codes = code_ref[0].astype(F32)
     own[...] = codes
     edge_l[...] = codes[0:2]
     edge_r[...] = codes[COLS - 2 : COLS]
+
+    pl.semaphore_wait(barrier, PLANE - 1 + LINE - 1 + 2)
+
+    to_right = pltpu.make_async_remote_copy(
+        edge_r, halo_l, halo_send_sem.at[0], halo_recv_sem.at[0], device_id=right, device_id_type=MESH
+    )
+    to_left = pltpu.make_async_remote_copy(
+        edge_l, halo_r, halo_send_sem.at[1], halo_recv_sem.at[1], device_id=left, device_id_type=MESH
+    )
+    to_right.start()
+    to_left.start()
+
+    for arrival in arrivals[1:]:
+        arrival.wait()
 
     place, channel = iota((CH, CH), 0), iota((CH, CH), 1)
     perm = (channel == place % 32 // 4 * 12 + place // 32 * 4 + place % 4).astype(BF16)
@@ -121,17 +150,6 @@
             w2t[pl.ds(back * CH, CH), :] = dot_t(eye, w2p[pl.ds(at * CH, CH), :]).astype(BF16)
     ahead_w[...] = dot_t(eye, w2p[...]).astype(BF16)
     back_w[...] = dot_t(eye, w2t[...]).astype(BF16)
-
-    pl.semaphore_wait(barrier, PLANE - 1 + LINE - 1 + 2)
-
-    to_right = pltpu.make_async_remote_copy(
-        edge_r, halo_l, halo_send_sem.at[0], halo_recv_sem.at[0], device_id=right, device_id_type=MESH
-    )
-    to_left = pltpu.make_async_remote_copy(
-        edge_l, halo_r, halo_send_sem.at[1], halo_recv_sem.at[1], device_id=left, device_id_type=MESH
-    )
-    to_right.start()
-    to_left.start()
 
     level = jnp.where(iota((8, 1), 0) < 3, 8.0, 5.0)
     p8[...] = jnp.zeros_like(p8)
@@ -188,10 +206,10 @@
         digits[c] = jnp.concatenate(block + [jnp.zeros_like(value)], axis=0).astype(BF16)
     digits[COLS + 4 : COLS + 8] = jnp.zeros((4, 32, ROWS), BF16)
 
-    gram = None
-    for c in range(COLS):
-        term = dot_t(digits[c + 2], digits[c + 2 : c + 6].reshape(128, ROWS))
-        gram = term if gram is None else gram + term
+    gram = dot_t(
+        jnp.concatenate([digits[c + 2] for c in range(COLS)], axis=1),
+        jnp.concatenate([digits[c + 2 : c + 6].reshape(128, ROWS) for c in range(COLS)], axis=1),
+    )
     for j in range(PLANE):
         gs[j] = gram[j : j + 1]
     for j in range(PLANE):
@@ -200,11 +218,13 @@
             send(gs.at[j], g_rs.at[q], 0, plane(j)).start()
     g_rs[q] = gs[q]
 
-    def grad_step(c, carry):
-        grads[c] = dot(back_w[...], cots[pl.ds(c, 3)].reshape(9 * CH, ROWS))
+    def grad_step(step, carry):
+        for k in range(6):
+            c = step * 6 + k
+            grads[c] = dot(back_w[...], cots[pl.ds(c, 3)].reshape(9 * CH, ROWS))
         return carry
 
-    lax.fori_loop(0, 6, grad_step, 0)
+    lax.fori_loop(0, 3, grad_step, 0)
     some = send(gs.at[pl.ds(0, PLANE - 1)], g_rs.at[pl.ds(0, PLANE - 1)], 0, right)
     some.wait()
     g_z[z] = jnp.sum(g_rs[...], axis=0)
@@ -212,14 +232,12 @@
         @pl.when(z != j)
         def _():
             send(g_z.at[z], g_z.at[z], 1, line(j)).start()
-    lax.fori_loop(6, 12, grad_step, 0)
     send(g_z.at[pl.ds(0, LINE - 1)], g_z.at[pl.ds(0, LINE - 1)], 1, right).wait()
     g_ag[q] = jnp.sum(g_z[...], axis=0)
     for j in range(PLANE):
         @pl.when(q != j)
         def _():
             send(g_ag.at[q], g_ag.at[q], 2, plane(j)).start()
-    lax.fori_loop(12, 18, grad_step, 0)
     send(g_ag.at[pl.ds(0, PLANE - 1)], g_ag.at[pl.ds(0, PLANE - 1)], 2, right).wait()
     for j in range(PLANE):
         g_all[j : j + 1, :] = g_ag[j]
@@ -261,32 +279,28 @@
         [dot_t(perm, part.astype(BF16)) for part in pieces(pre_w, 2)], axis=0
     ).astype(BF16)
 
-    def act_step(c, total):
-        taps = digits[pl.ds(c, 3)].reshape(CH, ROWS)
-        both = dot(pre_w, taps)
-        pre = both[0:CH] + both[CH : 2 * CH]
-        sigma = 0.5 * jnp.tanh(0.5 * pre) + 0.5
-        act = pre * sigma
-        slope = sigma + act * (1.0 - sigma)
-        acts[c, 0] = later(act, wide).astype(BF16)
-        acts[c, 1] = act.astype(BF16)
-        acts[c, 2] = earlier(act, wide).astype(BF16)
-        return total + dot_t(taps, (grads[c] * slope).astype(BF16))
-
-    total = lax.fori_loop(0, COLS + 2, act_step, jnp.zeros((CH, CH), F32))
+    def act_step(step, total):
+        for k in range(9):
+            c = step * 9 + k
+            taps = digits[pl.ds(c, 3)].reshape(CH, ROWS)
+            both = dot(pre_w, taps)
+            pre = both[0:CH] + both[CH : 2 * CH]
+            sigma = 0.5 * jnp.tanh(0.5 * pre) + 0.5
+            act = pre * sigma
+            slope = sigma + act * (1.0 - sigma)
+            acts[c, 0] = later(act, wide).astype(BF16)
+            acts[c, 1] = act.astype(BF16)
+            acts[c, 2] = earlier(act, wide).astype(BF16)
+            total = total + dot_t(taps, (grads[c] * slope).astype(BF16))
+        return total
+
+    total = lax.fori_loop(0, 2, act_step, jnp.zeros((CH, CH), F32))
     af[...] = jnp.zeros_like(af)
     af[0:CH, 0:CH] = dot32(total, perm.astype(F32))
 
-    sg[...] = jnp.zeros_like(sg)
-
-    def second_step(c, total):
-        value = cot_ref[c]
-        sg[:, 0:CH] += dot_t(acts[pl.ds(c, 3)].reshape(9 * CH, ROWS), value)
-        return total + dot_t(digits[c + 2], value)
-
-    cot_sum = lax.fori_loop(0, COLS, second_step, jnp.zeros((32, CH), F32))
+    cot_all = jnp.concatenate([cot_ref[c] for c in range(COLS)], axis=1)
+    cot_sum = dot_t(jnp.concatenate([digits[c + 2] for c in range(COLS)], axis=1), cot_all)
     af[CH : CH + 8, 0:CH] = cot_sum[8:16]
-    sg_send[...] = sg[...].reshape(CHUNKS, 32, 128).astype(BF16)
     for j in range(PLANE - 1):
         af_send[j] = af[unit_row(j) : unit_row(j) + 2, :]
     af_send[PLANE - 1] = jnp.zeros((2, 128), F32)
@@ -294,23 +308,34 @@
     for j in range(PLANE):
         @pl.when(q != j)
         def _():
-            if j < CHUNKS:
+            send(af_send.at[j], af_recv.at[q], 4, plane(j)).start()
+    sg_send[:, :, CH:128] = jnp.zeros((CHUNKS, 32, 128 - CH), BF16)
+    for dc in range(3):
+        taps = [acts[c + dc].reshape(3 * CH, ROWS) for c in range(COLS)]
+        got = dot_t(jnp.concatenate(taps, axis=1), cot_all)
+        sg_send[9 * dc : 9 * dc + 9, :, 0:CH] = got.reshape(9, 32, CH).astype(BF16)
+        for j in range(9 * dc, 9 * dc + 9):
+            @pl.when(q != j)
+            def _():
                 send(sg_send.at[j], sg_recv.at[q], 3, plane(j)).start()
-            send(af_send.at[j], af_recv.at[q], 4, plane(j)).start()
     af_recv[q] = af_send[q]
 
     @pl.when(q < CHUNKS)
     def _():
         sg_recv[q] = sg_send[q]
 
-    def mixed_step(c, carry):
-        out = dot(ahead_w[...], acts[pl.ds(c, 3)].reshape(9 * CH, ROWS))
-        lift = dot(lift_w, digits[c + 2])
-        lift = (lift[0:CH] + lift[CH : 2 * CH]) + lift[2 * CH : 3 * CH]
-        mixed_ref[c] = (lift.astype(BF16).astype(F32) + out).astype(BF16)
+    def mixed_step(step, carry):
+        for k in range(8):
+            c = step * 8 + k
+            out = dot(ahead_w[...], acts[pl.ds(c, 3)].reshape(9 * CH, ROWS))
+            lift = dot(lift_w, digits[c + 2])
+            lift = (lift[0:CH] + lift[CH : 2 * CH]) + lift[2 * CH : 3 * CH]
+            mixed_ref[c] = (lift.astype(BF16).astype(F32) + out).astype(BF16)
         return carry
 
-    lax.fori_loop(0, 6, mixed_step, 0)
+    lax.fori_loop(0, 2, mixed_step, 0)
+    departure = pltpu.make_async_copy(mixed_ref, mixed_out, out_sem)
+    departure.start()
     z_send[...] = jnp.zeros_like(z_send)
 
     @pl.when(q < CHUNKS)
@@ -339,14 +364,12 @@
         def _():
             send(z_send.at[j % BANDS], z_recv.at[z], 5, line(j)).start()
     z_recv[z] = z_send[band]
-    lax.fori_loop(6, 12, mixed_step, 0)
     send(z_recv.at[pl.ds(0, LINE - 1)], z_recv.at[pl.ds(0, LINE - 1)], 5, right).wait()
     ag[q] = jnp.sum(z_recv[...], axis=0)
     for j in range(PLANE):
         @pl.when(q != j)
         def _():
             send(ag.at[q], ag.at[q], 6, plane(j)).start()
-    lax.fori_loop(12, COLS, mixed_step, 0)
     send(ag.at[pl.ds(0, PLANE - 1)], ag.at[pl.ds(0, PLANE - 1)], 6, right).wait()
 
     for j in range(CHUNKS):
@@ -378,12 +401,50 @@
             back_sum = term if back_sum is None else back_sum + term
     back_sum = back_sum[0:8] + back_sum[8:16] + back_sum[16:24] + af[CH : CH + 8, 0:CH]
     proj_out[...] = (back_sum / level)[0:6]
+    departure.wait()
+
+
+def write_out(*refs):
+    sources, targets, held = refs[0:6], refs[6:12], refs[12:18]
+    in_sem, out_sem = refs[18], refs[19]
+    parts = [(0, pl.ds(4 * k, 4)) for k in range(4)] + [(k, None) for k in range(1, 6)]
+
+    def view(group, part):
+        which, rows = part
+        return group[which] if rows is None else group[which].at[rows]
+
+    ins = [
+        pltpu.make_async_copy(view(sources, part), view(held, part), in_sem.at[k])
+        for k, part in enumerate(parts)
+    ]
+    outs = [
+        pltpu.make_async_copy(view(held, part), view(targets, part), out_sem.at[k])
+        for k, part in enumerate(parts)
+    ]
+    for copy in ins:
+        copy.start()
+    for arrived, copy in zip(ins, outs):
+        arrived.wait()
+        copy.start()
+    for copy in outs:
+        copy.wait()
 
 
 def body(code_ids, projection, first_weight, second_weight, norm_gain, norm_shift, cotangent):
     shape = jax.ShapeDtypeStruct
     vmem = pl.BlockSpec(memory_space=pltpu.VMEM)
-    scratch = [
+    anywhere = pl.BlockSpec(memory_space=pltpu.HBM)
+    operands = [
+        jnp.swapaxes(code_ids, 1, 2),
+        projection,
+        first_weight,
+        second_weight,
+        norm_gain.reshape(1, CH),
+        norm_shift.reshape(1, CH),
+        cotangent,
+    ]
+    scratch = [pltpu.VMEM(operand.shape, operand.dtype) for operand in operands] + [
+        pltpu.VMEM((COLS, CH, ROWS), BF16),
         pltpu.VMEM((COLS, ROWS), F32),
         pltpu.VMEM((2, ROWS), F32), pltpu.VMEM((2, ROWS), F32),
         pltpu.VMEM((2, ROWS), F32), pltpu.VMEM((2, ROWS), F32),
@@ -397,43 +458,45 @@
         pltpu.VMEM((PLANE, 1, 128), F32), pltpu.VMEM((PLANE, 1, 128), F32),
         pltpu.VMEM((LINE, 1, 128), F32), pltpu.VMEM((PLANE, 1, 128), F32),
         pltpu.VMEM((128, 128), F32),
-        pltpu.VMEM((9 * CH, 128), F32),
         pltpu.VMEM((CHUNKS, 32, 128), BF16), pltpu.VMEM((PLANE, 32, 128), BF16),
         pltpu.VMEM((CH + 8, 128), F32),
         pltpu.VMEM((PLANE, 2, 128), F32), pltpu.VMEM((PLANE, 2, 128), F32),
         pltpu.VMEM((BANDS, 8, 128), F32), pltpu.VMEM((LINE, 8, 128), F32),
         pltpu.VMEM((PLANE, 8, 128), F32),
+        pltpu.SemaphoreType.DMA((7,)), pltpu.SemaphoreType.DMA,
         pltpu.SemaphoreType.DMA((2,)), pltpu.SemaphoreType.DMA((2,)),
         pltpu.SemaphoreType.DMA((7,)), pltpu.SemaphoreType.DMA((7,)),
     ]
-    mixed, first, second, gain_grad, shift_grad, proj = pl.pallas_call(
+    outputs = [
+        shape((COLS, CH, ROWS), BF16),
+        shape((9, 12, CH), F32),
+        shape((9, 12, CH), F32),
+        shape((1, CH), F32),
+        shape((1, CH), F32),
+        shape((6, CH), F32),
+    ]
+    results = pl.pallas_call(
         kernel,
-        out_shape=[
-            shape((COLS, CH, ROWS), BF16),
-            shape((9, 12, CH), F32),
-            shape((9, 12, CH), F32),
-            shape((1, CH), F32),
-            shape((1, CH), F32),
-            shape((6, CH), F32),
-        ],
-        in_specs=[vmem] * 7,
-        out_specs=[vmem] * 6,
+        out_shape=outputs,
+        in_specs=[anywhere] * 7,
+        out_specs=[anywhere] + [vmem] * 5,
         scratch_shapes=scratch,
         compiler_params=pltpu.CompilerParams(
-            collective_id=0, has_side_effects=True, vmem_limit_bytes=40 * 1024 * 1024
+            collective_id=0, has_side_effects=True, vmem_limit_bytes=VMEM_BYTES
         ),
         cost_estimate=pl.CostEstimate(
             flops=2_500_000_000, bytes_accessed=2_500_000, transcendentals=450_000
         ),
-    )(
-        code_ids,
-        projection,
-        first_weight,
-        second_weight,
-        norm_gain.reshape(1, CH),
-        norm_shift.reshape(1, CH),
-        cotangent,
-    )
+    )(*operands)
+    mixed, first, second, gain_grad, shift_grad, proj = pl.pallas_call(
+        write_out,
+        out_shape=outputs,
+        in_specs=[anywhere] * 6,
+        out_specs=[anywhere] * 6,
+        scratch_shapes=[pltpu.VMEM(output.shape, output.dtype) for output in outputs]
+        + [pltpu.SemaphoreType.DMA((9,)), pltpu.SemaphoreType.DMA((9,))],
+        compiler_params=pltpu.CompilerParams(vmem_limit_bytes=VMEM_BYTES),
+    )(*results)
     return mixed, first, second, gain_grad.reshape(CH), shift_grad.reshape(CH), proj
 
 

time: 82 us -> 71 us (0.87)
  local copies, waits for them, and re-layouts: 7.61 us -> 0 us
  Pallas kernels: 73.4 us -> 70.2 us
    unnamed x19 -> x0, local copies, waits for them, and re-layouts: 7.61 us -> none
    pallas_call x1 -> x2, Pallas kernels: 73.4 us -> 70.2 us  [the longest x1 68.1 us: body(): pl.pallas_call(kernel, out_shape=outputs, in_specs=[anywhere] * 7, out_sp...]
where the time goes in v2:
time: 71 us; the launch traced here: 70.8 us
  Pallas kernels  70.2 us (99%)
    pallas_call x1, Pallas kernels, body(): pl.pallas_call(kernel, out_shape=outputs, in_specs=[anywhere] * 7, out_sp...  68.1 us
    pallas_call x1, Pallas kernels, body(): pl.pallas_call(write_out, out_shape=outputs, in_specs=[anywhere] * 6, out...  2.09 us

profile of v2, /device:TPU:1, one launch (start us, length us, event | category | flops | bytes accessed | tf_op | source)
XLA Modules:
  0.0 70.8 jit_solution(3105567504202106864)
XLA Ops:
  0.6 68.1 %shard_map.118 = (bf16[16,96,256]{2,1,0:T(8,128)(2,1)}, f32[9,12,96]{2,1,0:T(8,128)}, f32[9,12,96]{2,1,0:T(8,128)}, f32[1,96]{1,0:T(1,128)}, f32[1,96]{1,0:T(1,128)}, /*index=5*/f32[6,96]{1,0:T(8,128)}) custom-call(s32[1,16,256]{2,1,0:T(8,128)} %bitcast.5, f32[6,96]{1,0:T(8,128)} %proj_in.1, bf16[9,96,96]{2,1,0:T(8,128)(2,1)} %w1_in.1, ...), custom_call_target="tpu_custom_call" | custom-call | flops 2500000000 | bytes 2500000 | tf_op jit(solution)/shard_map/pallas_call | solution.py:478
  68.7 2.1 %shard_map.119 = (bf16[16,96,256]{2,1,0:T(8,128)(2,1)}, f32[9,12,96]{2,1,0:T(8,128)}, f32[9,12,96]{2,1,0:T(8,128)}, f32[1,96]{1,0:T(1,128)}, f32[1,96]{1,0:T(1,128)}, /*index=5*/f32[6,96]{1,0:T(8,128)}) custom-call(bf16[16,96,256]{2,1,0:T(8,128)(2,1)} %get-tuple-element.18.refs_0_, f32[9,12,96]{2,1,0:T(8,128)} %get-tuple-element.19.refs_1_, ...), custom_call_target="tpu_custom_call" | custom-call | tf_op jit(solution)/shard_map/pallas_call | solution.py:491

commit v3 on v2

--- a/solution.py
+++ b/solution.py
@@ -13,6 +13,17 @@
 PLANE, LINE, BANDS = 32, 16, 8
 CHUNKS = 27
 POSITIONS = float(2**21)
+
+
+def hops(step, ring):
+    return min(step, ring - step)
+
+
+PLANE_OFFSETS = sorted(
+    [(dy, dx, dc) for dy in range(4) for dx in range(4) for dc in range(2) if dy + dx + dc > 0],
+    key=lambda step: -4 * hops(step[0], 4) - 4 * hops(step[1], 4) - step[2],
+)
+LINE_OFFSETS = sorted(range(1, LINE), key=lambda step: -hops(step, LINE))
 VMEM_BYTES = 64 * 1024 * 1024 - 65536
 ONE = 46
 
@@ -68,12 +79,49 @@
     code_in, proj_in, w1_in, w2_in, gain_in, shift_in, cot_in,
     mixed_out, first_ref, second_ref, gain_out, shift_out, proj_out,
     code_ref, proj_ref, w1_ref, w2_ref, gain_ref, shift_ref, cot_ref, mixed_ref,
-    own, edge_l, edge_r, halo_l, halo_r,
+    own, edge_l, edge_r, halo_l, halo_r, mid_l, mid_r, seam,
     digits, cots, acts, grads, w2p, w2t, back_w, ahead_w, p8, wt,
     gs, g_rs, g_z, g_ag, g_all,
     sg_send, sg_recv, af, af_send, af_recv, z_send, z_recv, ag,
     in_sem, out_sem, halo_send_sem, halo_recv_sem, send_sem, recv_sem,
 ):
+    face, band = lax.axis_index("face"), lax.axis_index("band")
+    core, z_hi, yx = face % 2, face // 2 % 2, face // 4
+    y, x = yx // 4, yx % 4
+    q, z = yx * 2 + core, z_hi * BANDS + band
+
+    def plane(j):
+        return (j // 2 * 4 + z_hi * 2 + j % 2, band)
+
+    def line(j):
+        return (yx * 4 + j // BANDS * 2 + core, j % BANDS)
+
+    mates = [
+        ((y + dy) % 4 * 4 + (x + dx) % 4) * 2 + (core + dc) % 2 for dy, dx, dc in PLANE_OFFSETS
+    ]
+    others = [(z + dz) % LINE for dz in LINE_OFFSETS]
+
+    left, right = ((face + 63) % 64, band), ((face + 1) % 64, band)
+
+    def half_way(seam_face):
+        there = (seam_face // 2 % 2 * BANDS + band + 4) % LINE
+        return (seam_face // 4 * 4 + there // BANDS * 2 + 1, there % BANDS)
+
+    from_z = (z + 12) % LINE
+    from_right = ((yx * 4 + from_z // BANDS * 2 + 2) % 64, from_z % BANDS)
+
+    barrier = pltpu.get_barrier_semaphore()
+    for target in (left, right):
+        pl.semaphore_signal(barrier, 1, device_id=target, device_id_type=MESH)
+    @pl.when(core == 1)
+    def _():
+        pl.semaphore_signal(barrier, 1, device_id=from_right, device_id_type=MESH)
+
+    for j in others:
+        pl.semaphore_signal(barrier, 1, device_id=line(j), device_id_type=MESH)
+    for j in mates:
+        pl.semaphore_signal(barrier, 1, device_id=plane(j), device_id_type=MESH)
+
     arrivals = [
         pltpu.make_async_copy(source, target, in_sem.at[k])
         for k, (source, target) in enumerate(
@@ -86,30 +134,6 @@
     for arrival in arrivals:
         arrival.start()
 
-    face, band = lax.axis_index("face"), lax.axis_index("band")
-    core, z_hi, yx = face % 2, face // 2 % 2, face // 4
-    q, z = yx * 2 + core, z_hi * BANDS + band
-
-    def plane(j):
-        return (j // 2 * 4 + z_hi * 2 + j % 2, band)
-
-    def line(j):
-        return (yx * 4 + j // BANDS * 2 + core, j % BANDS)
-
-    left, right = ((face + 63) % 64, band), ((face + 1) % 64, band)
-
-    barrier = pltpu.get_barrier_semaphore()
-    for target in (left, right):
-        pl.semaphore_signal(barrier, 1, device_id=target, device_id_type=MESH)
-    for j in range(PLANE):
-        @pl.when(q != j)
-        def _():
-            pl.semaphore_signal(barrier, 1, device_id=plane(j), device_id_type=MESH)
-    for j in range(LINE):
-        @pl.when(z != j)
-        def _():
-            pl.semaphore_signal(barrier, 1, device_id=line(j), device_id_type=MESH)
-
     def send(src, dst, sem, target):
         return pltpu.make_async_remote_copy(
             src, dst, send_sem.at[sem], recv_sem.at[sem], device_id=target, device_id_type=MESH
@@ -124,7 +148,7 @@
     edge_l[...] = codes[0:2]
     edge_r[...] = codes[COLS - 2 : COLS]
 
-    pl.semaphore_wait(barrier, PLANE - 1 + LINE - 1 + 2)
+    pl.semaphore_wait(barrier, PLANE - 1 + LINE - 1 + 2 + 1 - core)
 
     to_right = pltpu.make_async_remote_copy(
         edge_r, halo_l, halo_send_sem.at[0], halo_recv_sem.at[0], device_id=right, device_id_type=MESH
@@ -132,8 +156,25 @@
     to_left = pltpu.make_async_remote_copy(
         edge_l, halo_r, halo_send_sem.at[1], halo_recv_sem.at[1], device_id=left, device_id_type=MESH
     )
+    mid_right = pltpu.make_async_remote_copy(
+        edge_r, mid_l, halo_send_sem.at[2], halo_recv_sem.at[2],
+        device_id=half_way(face), device_id_type=MESH,
+    )
+    mid_left = pltpu.make_async_remote_copy(
+        edge_l, mid_r, halo_send_sem.at[3], halo_recv_sem.at[3],
+        device_id=half_way((face + 63) % 64), device_id_type=MESH,
+    )
+
+    @pl.when(core == 1)
+    def _():
+        mid_right.start()
+
+    @pl.when(core == 0)
+    def _():
+        mid_left.start()
+
+    to_left.start()
     to_right.start()
-    to_left.start()
 
     for arrival in arrivals[1:]:
         arrival.wait()
@@ -184,39 +225,75 @@
 
     lax.fori_loop(0, COLS, cot_step, 0)
 
-    to_right.wait()
-    to_left.wait()
-
     index = iota((8, 1), 0)
     stride = jnp.where(
         index == 0, 1.0, jnp.where(index == 1, 8.0, jnp.where(index == 2, 64.0,
         jnp.where(index == 3, 512.0, jnp.where(index == 4, 2560.0, 12800.0)))))
     per_stride, per_level = 1.0 / stride, 1.0 / level
-    for c in range(COLS + 4):
-        if c < 2:
-            row = halo_l[c : c + 1, :]
-        elif c < COLS + 2:
-            row = own[c - 2 : c - 1, :]
-        else:
-            row = halo_r[c - COLS - 2 : c - COLS - 1, :]
+
+    def decode(row):
         quotient = jnp.floor((row + 0.5) * per_stride)
         digit = quotient - level * jnp.floor((quotient + 0.5) * per_level)
         value = jnp.where(index < 6, 2.0 * digit - (level - 1.0), 0.0)
         block = [later(value, lane), jnp.where(index == 6, 1.0, value), earlier(value, lane)]
-        digits[c] = jnp.concatenate(block + [jnp.zeros_like(value)], axis=0).astype(BF16)
-    digits[COLS + 4 : COLS + 8] = jnp.zeros((4, 32, ROWS), BF16)
+        return jnp.concatenate(block + [jnp.zeros_like(value)], axis=0).astype(BF16)
+
+    for c in range(COLS):
+        digits[c + 2] = decode(own[c : c + 1, :])
+
+    @pl.when(core == 0)
+    def _():
+        to_left.wait_recv()
+        seam[0:2, :] = own[COLS - 2 : COLS, :]
+        seam[2:4, :] = halo_r[...]
+
+    @pl.when(core == 1)
+    def _():
+        mid_right.wait_recv()
+        mid_left.wait_recv()
+        seam[0:2, :] = mid_l[...]
+        seam[2:4, :] = mid_r[...]
+
+    beside = [decode(seam[c : c + 1, :]) for c in range(4)]
+
+    none = jnp.zeros((32, ROWS), BF16)
+
+    def ahead(c):
+        return jnp.concatenate(
+            [digits[c + 2 + d] if c + d < COLS else none for d in range(3)] + [none], axis=0
+        )
 
     gram = dot_t(
-        jnp.concatenate([digits[c + 2] for c in range(COLS)], axis=1),
-        jnp.concatenate([digits[c + 2 : c + 6].reshape(128, ROWS) for c in range(COLS)], axis=1),
+        jnp.concatenate([digits[c + 2] for c in range(COLS)] + beside[0:2], axis=1),
+        jnp.concatenate(
+            [ahead(c) for c in range(COLS)]
+            + [
+                jnp.concatenate([none, none, beside[2], none], axis=0),
+                jnp.concatenate([none, beside[2], beside[3], none], axis=0),
+            ],
+            axis=1,
+        ),
     )
     for j in range(PLANE):
         gs[j] = gram[j : j + 1]
-    for j in range(PLANE):
-        @pl.when(q != j)
-        def _():
-            send(gs.at[j], g_rs.at[q], 0, plane(j)).start()
+    for j in mates:
+        send(gs.at[j], g_rs.at[q], 0, plane(j)).start()
     g_rs[q] = gs[q]
+
+    @pl.when(core == 1)
+    def _():
+        to_left.wait_recv()
+        mid_right.wait_send()
+
+    @pl.when(core == 0)
+    def _():
+        mid_left.wait_send()
+
+    to_left.wait_send()
+    to_right.wait()
+    for c in range(2):
+        digits[c] = decode(halo_l[c : c + 1, :])
+        digits[COLS + 2 + c] = decode(halo_r[c : c + 1, :])
 
     def grad_step(step, carry):
         for k in range(6):
@@ -228,16 +305,12 @@
     some = send(gs.at[pl.ds(0, PLANE - 1)], g_rs.at[pl.ds(0, PLANE - 1)], 0, right)
     some.wait()
     g_z[z] = jnp.sum(g_rs[...], axis=0)
-    for j in range(LINE):
-        @pl.when(z != j)
-        def _():
-            send(g_z.at[z], g_z.at[z], 1, line(j)).start()
+    for j in others:
+        send(g_z.at[z], g_z.at[z], 1, line(j)).start()
     send(g_z.at[pl.ds(0, LINE - 1)], g_z.at[pl.ds(0, LINE - 1)], 1, right).wait()
     g_ag[q] = jnp.sum(g_z[...], axis=0)
-    for j in range(PLANE):
-        @pl.when(q != j)
-        def _():
-            send(g_ag.at[q], g_ag.at[q], 2, plane(j)).start()
+    for j in mates:
+        send(g_ag.at[q], g_ag.at[q], 2, plane(j)).start()
     send(g_ag.at[pl.ds(0, PLANE - 1)], g_ag.at[pl.ds(0, PLANE - 1)], 2, right).wait()
     for j in range(PLANE):
         g_all[j : j + 1, :] = g_ag[j]
@@ -305,10 +378,8 @@
         af_send[j] = af[unit_row(j) : unit_row(j) + 2, :]
     af_send[PLANE - 1] = jnp.zeros((2, 128), F32)
 
-    for j in range(PLANE):
-        @pl.when(q != j)
-        def _():
-            send(af_send.at[j], af_recv.at[q], 4, plane(j)).start()
+    for j in mates:
+        send(af_send.at[j], af_recv.at[q], 4, plane(j)).start()
     sg_send[:, :, CH:128] = jnp.zeros((CHUNKS, 32, 128 - CH), BF16)
     for dc in range(3):
         taps = [acts[c + dc].reshape(3 * CH, ROWS) for c in range(COLS)]
@@ -359,17 +430,13 @@
     for b in range(BANDS):
         z_send[b, 4:6] = af_sum
 
-    for j in range(LINE):
-        @pl.when(z != j)
-        def _():
-            send(z_send.at[j % BANDS], z_recv.at[z], 5, line(j)).start()
+    for j in others:
+        send(z_send.at[j % BANDS], z_recv.at[z], 5, line(j)).start()
     z_recv[z] = z_send[band]
     send(z_recv.at[pl.ds(0, LINE - 1)], z_recv.at[pl.ds(0, LINE - 1)], 5, right).wait()
     ag[q] = jnp.sum(z_recv[...], axis=0)
-    for j in range(PLANE):
-        @pl.when(q != j)
-        def _():
-            send(ag.at[q], ag.at[q], 6, plane(j)).start()
+    for j in mates:
+        send(ag.at[q], ag.at[q], 6, plane(j)).start()
     send(ag.at[pl.ds(0, PLANE - 1)], ag.at[pl.ds(0, PLANE - 1)], 6, right).wait()
 
     for j in range(CHUNKS):
@@ -448,7 +515,8 @@
         pltpu.VMEM((COLS, ROWS), F32),
         pltpu.VMEM((2, ROWS), F32), pltpu.VMEM((2, ROWS), F32),
         pltpu.VMEM((2, ROWS), F32), pltpu.VMEM((2, ROWS), F32),
-        pltpu.VMEM((COLS + 8, 32, ROWS), BF16),
+        pltpu.VMEM((2, ROWS), F32), pltpu.VMEM((2, ROWS), F32), pltpu.VMEM((4, ROWS), F32),
+        pltpu.VMEM((COLS + 4, 32, ROWS), BF16),
         pltpu.VMEM((COLS + 4, 3, CH, ROWS), BF16),
         pltpu.VMEM((COLS + 2, 3, CH, ROWS), BF16),
         pltpu.VMEM((COLS + 2, CH, ROWS), F32),
@@ -464,7 +532,7 @@
         pltpu.VMEM((BANDS, 8, 128), F32), pltpu.VMEM((LINE, 8, 128), F32),
         pltpu.VMEM((PLANE, 8, 128), F32),
         pltpu.SemaphoreType.DMA((7,)), pltpu.SemaphoreType.DMA,
-        pltpu.SemaphoreType.DMA((2,)), pltpu.SemaphoreType.DMA((2,)),
+        pltpu.SemaphoreType.DMA((4,)), pltpu.SemaphoreType.DMA((4,)),
         pltpu.SemaphoreType.DMA((7,)), pltpu.SemaphoreType.DMA((7,)),
     ]
     outputs = [

time: 71 us -> 68.6 us (0.966)
  Pallas kernels: 70.2 us -> 67.8 us
    pallas_call x1, Pallas kernels: 68.1 us -> 65.7 us  [body(): pl.pallas_call(kernel, out_shape=outputs, in_specs=[anywhere] * 7, out_sp...]
where the time goes in v3:
time: 68.6 us; the launch traced here: 68.4 us
  Pallas kernels  67.8 us (99%)
    pallas_call x1, Pallas kernels, body(): pl.pallas_call(kernel, out_shape=outputs, in_specs=[anywhere] * 7, out_sp...  65.7 us
    pallas_call x1, Pallas kernels, body(): pl.pallas_call(write_out, out_shape=outputs, in_specs=[anywhere] * 6, out...  2.09 us

profile of v3, /device:TPU:1, one launch (start us, length us, event | category | flops | bytes accessed | tf_op | source)
XLA Modules:
  0.0 68.4 jit_solution(8435717041789545467)
XLA Ops:
  0.6 65.7 %shard_map.118 = (bf16[16,96,256]{2,1,0:T(8,128)(2,1)}, f32[9,12,96]{2,1,0:T(8,128)}, f32[9,12,96]{2,1,0:T(8,128)}, f32[1,96]{1,0:T(1,128)}, f32[1,96]{1,0:T(1,128)}, /*index=5*/f32[6,96]{1,0:T(8,128)}) custom-call(s32[1,16,256]{2,1,0:T(8,128)} %bitcast.5, f32[6,96]{1,0:T(8,128)} %proj_in.1, bf16[9,96,96]{2,1,0:T(8,128)(2,1)} %w1_in.1, ...), custom_call_target="tpu_custom_call" | custom-call | flops 2500000000 | bytes 2500000 | tf_op jit(solution)/shard_map/pallas_call | solution.py:546
  66.4 2.1 %shard_map.119 = (bf16[16,96,256]{2,1,0:T(8,128)(2,1)}, f32[9,12,96]{2,1,0:T(8,128)}, f32[9,12,96]{2,1,0:T(8,128)}, f32[1,96]{1,0:T(1,128)}, f32[1,96]{1,0:T(1,128)}, /*index=5*/f32[6,96]{1,0:T(8,128)}) custom-call(bf16[16,96,256]{2,1,0:T(8,128)(2,1)} %get-tuple-element.18.refs_0_, f32[9,12,96]{2,1,0:T(8,128)} %get-tuple-element.19.refs_1_, ...), custom_call_target="tpu_custom_call" | custom-call | tf_op jit(solution)/shard_map/pallas_call | solution.py:559

commit v4 on v3

--- a/solution.py
+++ b/solution.py
@@ -182,7 +182,6 @@
     place, channel = iota((CH, CH), 0), iota((CH, CH), 1)
     perm = (channel == place % 32 // 4 * 12 + place // 32 * 4 + place % 4).astype(BF16)
     eye = (channel == place).astype(BF16)
-    same_group = (channel // 3 == place // 3).astype(F32)
     for dc in range(3):
         for dr in range(3):
             tap, at = dr * 3 + dc, dc * 3 + dr
@@ -337,8 +336,15 @@
     weights = wt[...]
     spread = dot32(covariance, weights)
 
+    within = iota((8, 128), 1) % 3
+
     def by_group(value):
-        return dot32(jnp.broadcast_to(value, (8, CH)), same_group)[0:1]
+        row = jnp.concatenate([value, jnp.zeros((1, 128 - CH), F32)], axis=1)
+        row = jnp.broadcast_to(row, (8, 128))
+        next1, next2 = pltpu.roll(row, 127, 1), pltpu.roll(row, 126, 1)
+        last1, last2 = pltpu.roll(row, 1, 1), pltpu.roll(row, 2, 1)
+        first, middle, third = row + next1 + next2, last1 + row + next1, last2 + last1 + row
+        return jnp.where(within == 0, first, jnp.where(within == 1, middle, third))[0:1, 0:CH]
 
     channel_mean = jnp.sum(weights * digit_mean, axis=0, keepdims=True)
     mean = by_group(channel_mean) / 3.0
@@ -367,21 +373,21 @@
             total = total + dot_t(taps, (grads[c] * slope).astype(BF16))
         return total
 
-    total = lax.fori_loop(0, 2, act_step, jnp.zeros((CH, CH), F32))
-    af[...] = jnp.zeros_like(af)
-    af[0:CH, 0:CH] = dot32(total, perm.astype(F32))
-
+    total = act_step(1, act_step(0, jnp.zeros((CH, CH), F32)))
     cot_all = jnp.concatenate([cot_ref[c] for c in range(COLS)], axis=1)
-    cot_sum = dot_t(jnp.concatenate([digits[c + 2] for c in range(COLS)], axis=1), cot_all)
-    af[CH : CH + 8, 0:CH] = cot_sum[8:16]
-    for j in range(PLANE - 1):
-        af_send[j] = af[unit_row(j) : unit_row(j) + 2, :]
-    af_send[PLANE - 1] = jnp.zeros((2, 128), F32)
-
-    for j in mates:
-        send(af_send.at[j], af_recv.at[q], 4, plane(j)).start()
     sg_send[:, :, CH:128] = jnp.zeros((CHUNKS, 32, 128 - CH), BF16)
     for dc in range(3):
+        if dc == 2:
+            af[...] = jnp.zeros_like(af)
+            af[0:CH, 0:CH] = dot32(total, perm.astype(F32))
+
+            cot_sum = dot_t(jnp.concatenate([digits[c + 2] for c in range(COLS)], axis=1), cot_all)
+            af[CH : CH + 8, 0:CH] = cot_sum[8:16]
+            for j in range(PLANE - 1):
+                af_send[j] = af[unit_row(j) : unit_row(j) + 2, :]
+            af_send[PLANE - 1] = jnp.zeros((2, 128), F32)
+            for j in mates:
+                send(af_send.at[j], af_recv.at[q], 4, plane(j)).start()
         taps = [acts[c + dc].reshape(3 * CH, ROWS) for c in range(COLS)]
         got = dot_t(jnp.concatenate(taps, axis=1), cot_all)
         sg_send[9 * dc : 9 * dc + 9, :, 0:CH] = got.reshape(9, 32, CH).astype(BF16)
@@ -437,6 +443,9 @@
     ag[q] = jnp.sum(z_recv[...], axis=0)
     for j in mates:
         send(ag.at[q], ag.at[q], 6, plane(j)).start()
+    standard_sum = scale * (POSITIONS * spread + digit_sum * off)
+    chosen = iota((16, CH), 1) == band * 12 + iota((16, CH), 0)
+    proj_band = dot32_t(chosen.astype(F32), proj8)
     send(ag.at[pl.ds(0, PLANE - 1)], ag.at[pl.ds(0, PLANE - 1)], 6, right).wait()
 
     for j in range(CHUNKS):
@@ -453,11 +462,8 @@
     count = 3.0 * POSITIONS
     first_mean = by_group(gain * shift_grad) / count
     second_mean = by_group(gain * gain_grad) / count
-    standard_sum = scale * (POSITIONS * spread + digit_sum * off)
     grad_sum = scale * (gain * sums - first_mean * digit_sum - second_mean * standard_sum)
 
-    chosen = iota((16, CH), 1) == band * 12 + iota((16, CH), 0)
-    proj_band = dot32_t(chosen.astype(F32), proj8)
     back_sum = None
     for dc in range(3):
         for dr in range(3):
@@ -474,7 +480,7 @@
 def write_out(*refs):
     sources, targets, held = refs[0:6], refs[6:12], refs[12:18]
     in_sem, out_sem = refs[18], refs[19]
-    parts = [(0, pl.ds(4 * k, 4)) for k in range(4)] + [(k, None) for k in range(1, 6)]
+    parts = [(k, None) for k in range(1, 6)] + [(0, pl.ds(2 * k, 2)) for k in range(8)]
 
     def view(group, part):
         which, rows = part
@@ -562,7 +568,7 @@
         in_specs=[anywhere] * 6,
         out_specs=[anywhere] * 6,
         scratch_shapes=[pltpu.VMEM(output.shape, output.dtype) for output in outputs]
-        + [pltpu.SemaphoreType.DMA((9,)), pltpu.SemaphoreType.DMA((9,))],
+        + [pltpu.SemaphoreType.DMA((13,)), pltpu.SemaphoreType.DMA((13,))],
         compiler_params=pltpu.CompilerParams(vmem_limit_bytes=VMEM_BYTES),
     )(*results)
     return mixed, first, second, gain_grad.reshape(CH), shift_grad.reshape(CH), proj

time: 68.6 us -> 67.8 us (0.988)
  Pallas kernels: 67.8 us -> 66.9 us
    pallas_call x1, Pallas kernels: 65.7 us -> 64.8 us  [body(): pl.pallas_call(kernel, out_shape=outputs, in_specs=[anywhere] * 7, out_sp...]
where the time goes in v4:
time: 67.8 us; the launch traced here: 67.6 us
  Pallas kernels  66.9 us (99%)
    pallas_call x1, Pallas kernels, body(): pl.pallas_call(kernel, out_shape=outputs, in_specs=[anywhere] * 7, out_sp...  64.8 us
    pallas_call x1, Pallas kernels, body(): pl.pallas_call(write_out, out_shape=outputs, in_specs=[anywhere] * 6, out...  2.14 us

profile of v4, /device:TPU:1, one launch (start us, length us, event | category | flops | bytes accessed | tf_op | source)
XLA Modules:
  0.0 67.6 jit_solution(13162006050150183410)
XLA Ops:
  0.6 64.8 %shard_map.118 = (bf16[16,96,256]{2,1,0:T(8,128)(2,1)}, f32[9,12,96]{2,1,0:T(8,128)}, f32[9,12,96]{2,1,0:T(8,128)}, f32[1,96]{1,0:T(1,128)}, f32[1,96]{1,0:T(1,128)}, /*index=5*/f32[6,96]{1,0:T(8,128)}) custom-call(s32[1,16,256]{2,1,0:T(8,128)} %bitcast.5, f32[6,96]{1,0:T(8,128)} %proj_in.1, bf16[9,96,96]{2,1,0:T(8,128)(2,1)} %w1_in.1, ...), custom_call_target="tpu_custom_call" | custom-call | flops 2500000000 | bytes 2500000 | tf_op jit(solution)/shard_map/pallas_call | solution.py:552
  65.4 2.1 %shard_map.119 = (bf16[16,96,256]{2,1,0:T(8,128)(2,1)}, f32[9,12,96]{2,1,0:T(8,128)}, f32[9,12,96]{2,1,0:T(8,128)}, f32[1,96]{1,0:T(1,128)}, f32[1,96]{1,0:T(1,128)}, /*index=5*/f32[6,96]{1,0:T(8,128)}) custom-call(bf16[16,96,256]{2,1,0:T(8,128)(2,1)} %get-tuple-element.18.refs_0_, f32[9,12,96]{2,1,0:T(8,128)} %get-tuple-element.19.refs_1_, ...), custom_call_target="tpu_custom_call" | custom-call | tf_op jit(solution)/shard_map/pallas_call | solution.py:565

commit v5 on v4

--- a/solution.py
+++ b/solution.py
@@ -391,7 +391,9 @@
         taps = [acts[c + dc].reshape(3 * CH, ROWS) for c in range(COLS)]
         got = dot_t(jnp.concatenate(taps, axis=1), cot_all)
         sg_send[9 * dc : 9 * dc + 9, :, 0:CH] = got.reshape(9, 32, CH).astype(BF16)
-        for j in range(9 * dc, 9 * dc + 9):
+        for k in range(9):
+            j = 9 * dc + (q + k) % 9
+
             @pl.when(q != j)
             def _():
                 send(sg_send.at[j], sg_recv.at[q], 3, plane(j)).start()

time: 67.8 us -> 67.9 us (level)
  no operation moved by 1% of the time
where the time goes in v5:
time: 67.9 us; the launch traced here: 67.7 us
  Pallas kernels  67.1 us (99%)
    pallas_call x1, Pallas kernels, body(): pl.pallas_call(kernel, out_shape=outputs, in_specs=[anywhere] * 7, out_sp...  64.9 us
    pallas_call x1, Pallas kernels, body(): pl.pallas_call(write_out, out_shape=outputs, in_specs=[anywhere] * 6, out...  2.14 us

profile of v5, /device:TPU:1, one launch (start us, length us, event | category | flops | bytes accessed | tf_op | source)
XLA Modules:
  0.0 67.7 jit_solution(12653625066799787149)
XLA Ops:
  0.6 64.9 %shard_map.118 = (bf16[16,96,256]{2,1,0:T(8,128)(2,1)}, f32[9,12,96]{2,1,0:T(8,128)}, f32[9,12,96]{2,1,0:T(8,128)}, f32[1,96]{1,0:T(1,128)}, f32[1,96]{1,0:T(1,128)}, /*index=5*/f32[6,96]{1,0:T(8,128)}) custom-call(s32[1,16,256]{2,1,0:T(8,128)} %bitcast.5, f32[6,96]{1,0:T(8,128)} %proj_in.1, bf16[9,96,96]{2,1,0:T(8,128)(2,1)} %w1_in.1, ...), custom_call_target="tpu_custom_call" | custom-call | flops 2500000000 | bytes 2500000 | tf_op jit(solution)/shard_map/pallas_call | solution.py:554
  65.6 2.1 %shard_map.119 = (bf16[16,96,256]{2,1,0:T(8,128)(2,1)}, f32[9,12,96]{2,1,0:T(8,128)}, f32[9,12,96]{2,1,0:T(8,128)}, f32[1,96]{1,0:T(1,128)}, f32[1,96]{1,0:T(1,128)}, /*index=5*/f32[6,96]{1,0:T(8,128)}) custom-call(bf16[16,96,256]{2,1,0:T(8,128)(2,1)} %get-tuple-element.18.refs_0_, f32[9,12,96]{2,1,0:T(8,128)} %get-tuple-element.19.refs_1_, ...), custom_call_target="tpu_custom_call" | custom-call | tf_op jit(solution)/shard_map/pallas_call | solution.py:567
